TPU v7x, 256 devices: a whole 4x4x8 slice. The times are simulated.
256 devices in a mesh: cls: 4 (over y), ptcl: 64 (over x, z, core).
Axes of the slice: x: 4, y: 4, z: 8, core: 2. Of those that a mesh axis runs over, the one named last changes fastest.
Arguments:
- images: bfloat16 [8192, 8192], P('ptcl'), may hold values from -0.125 to 0.125
- bin_lists: int32 [8192, 2], P('ptcl'), may hold values from 0 to 63, all different within a row; in each aligned block of 128 rows (0 to 127, 128 to 255, ...) at most 8 rows name the same one
- precision: bfloat16 [8192], P('ptcl'), may hold values from 0.35 to 2048
- references: bfloat16 [4, 32768, 8192], P('cls', 'ptcl'), may hold values from -1.5 to 1.5
- line_index: int32 [4, 32768, 64], P('cls', 'ptcl'), may hold values from 0 to 127
- interp_blocks: bfloat16 [64, 128, 128], replicated, may hold values from -0.5 to 0.5
Outputs:
- class_prob: float32 [8192, 4], P('ptcl', 'cls')
- volume: float32 [4, 8192, 128], P('cls', 'ptcl')
Inputs may be any that keep to these rules, and one draw needn't show every extreme that they name: `bin_lists`: each particle names 2 different bins; among the particles of one index of ptcl no bin is named more than 8 times, and in some draws' devices some bin exactly 8 times.
All inputs are finite; a program needn't handle non-finite values.
Results may differ from a plain program's by a relative error of at most 0.0034.
Values may be sent and summed in bfloat16 or wider, within the bound.
A program may use at most 128 MiB of HBM per device.

v0:
```python
import jax
import jax.numpy as jnp
from jax import lax
from jax.sharding import PartitionSpec as P

VLINES = 8192


def joined(value, axis, join):
    pieces = jax.tree.map(lambda part: lax.all_gather(part, axis), value)
    head = jax.tree.map(lambda part: part[0], pieces)
    tail = jax.tree.map(lambda part: part[1:], pieces)
    running, _ = lax.scan(lambda running, piece: (join(running, piece), None), head, tail)
    return running


def slot_layout(bin_rows, peers, spaces):
    flat_bins = bin_rows.reshape(-1)
    onehot = (flat_bins[:, None] == jnp.arange(peers, dtype=jnp.int32)[None, :]).astype(jnp.int32)
    position = jnp.sum((jnp.cumsum(onehot, axis=0) - onehot) * onehot, axis=1)
    slot_id = flat_bins * spaces + position
    source = jnp.arange(flat_bins.shape[0], dtype=jnp.int32) // bin_rows.shape[1]
    filled = jnp.zeros((peers * spaces,), jnp.int32).at[slot_id].set(1)
    slot_src = jnp.zeros((peers * spaces,), jnp.int32).at[slot_id].set(source)
    return (filled, slot_src)


def combine(former, latter):
    maximum = jnp.maximum(former[0], latter[0])
    return (
        maximum,
        former[1] * jnp.exp(former[0] - maximum) + latter[1] * jnp.exp(latter[0] - maximum),
    )


def local(images, bin_lists, precision, references, line_index, interp_blocks):
    peers = lax.axis_size("ptcl")
    count_local, pixels = images.shape
    spaces = 2 * count_local * bin_lists.shape[1] // peers
    filled, slot_src = slot_layout(bin_lists, peers, spaces)
    occupied = filled.astype(jnp.bfloat16)
    send_scale = (precision[slot_src] * occupied).reshape(peers, spaces)
    ref_rows = references[0]
    per_bin = ref_rows.shape[0]
    half_norm = 0.5 * jnp.sum(jnp.square(ref_rows.astype(jnp.float32)), axis=1)
    send_rows = (images[slot_src] * occupied[:, None]).reshape(peers, spaces, pixels)
    received = lax.all_to_all(send_rows, "ptcl", split_axis=0, concat_axis=0, tiled=True)
    leading = received.shape[:2]
    pixel_rows = received.reshape(-1, pixels)
    products = lax.dot_general(
        pixel_rows, ref_rows, (((1,), (1,)), ((), ())), preferred_element_type=jnp.float32
    )
    scores = lax.all_to_all(send_scale, "ptcl", split_axis=0, concat_axis=0, tiled=True).reshape(
        -1
    ).astype(jnp.float32)[:, None] * (products - half_norm[None, :])
    highest = jnp.max(scores, axis=1)
    totals = jnp.sum(jnp.exp(scores - highest[:, None]), axis=1)
    got_rows, scores, highest, totals = (
        received,
        scores.reshape(leading + (per_bin,)),
        highest.reshape(leading),
        totals.reshape(leading),
    )
    back_top, back_total = (
        lax.all_to_all(highest, "ptcl", split_axis=0, concat_axis=0, tiled=True),
        lax.all_to_all(totals, "ptcl", split_axis=0, concat_axis=0, tiled=True),
    )
    back_top = back_top.reshape(-1)
    back_total = back_total.reshape(-1)
    owner_mask = (slot_src[:, None] == jnp.arange(count_local, dtype=jnp.int32)[None, :]) & (
        filled[:, None] > 0
    )
    own_top = jnp.max(jnp.where(owner_mask, back_top[:, None], -jnp.inf), axis=0)
    own_total = jnp.sum(
        jnp.where(
            owner_mask, back_total[:, None] * jnp.exp(back_top[:, None] - own_top[None, :]), 0.0
        ),
        axis=0,
    )
    all_top, all_total = joined((own_top, own_total), "cls", combine)
    log_total = all_top + jnp.log(all_total)
    class_prob = (own_total * jnp.exp(own_top - log_total))[:, None]
    slot_log = jnp.where(filled > 0, log_total[slot_src], 1e30).reshape(peers, spaces)
    got_log = lax.all_to_all(slot_log, "ptcl", split_axis=0, concat_axis=0, tiled=True)
    weights = (per_bin * jnp.exp(scores - got_log[:, :, None])).astype(jnp.bfloat16)
    class_image = lax.dot_general(
        weights.reshape(-1, per_bin),
        got_rows.reshape(-1, pixels),
        (((0,), (0,)), ((), ())),
        preferred_element_type=jnp.float32,
    ).astype(jnp.bfloat16)
    line_count, line_width = (interp_blocks.shape[0], interp_blocks.shape[1])
    band_width = VLINES // line_count
    band_onehot = (
        line_index[0][:, :, None] == jnp.arange(band_width, dtype=jnp.int32)[None, None, :]
    ).astype(jnp.bfloat16)
    band_sums = jnp.einsum(
        "rlw,rlk->lwk",
        band_onehot,
        class_image.reshape(per_bin, line_count, line_width),
        preferred_element_type=jnp.float32,
    )
    partial_volume = jnp.einsum(
        "lwk,lkj->lwj",
        band_sums,
        interp_blocks.astype(jnp.float32),
        precision=lax.Precision.HIGHEST,
    ).reshape(VLINES, line_width)
    volume = lax.psum_scatter(partial_volume, "ptcl", scatter_dimension=0, tiled=True)
    return (class_prob, volume[None])


def solution(mesh):
    in_specs = (
        P("ptcl", None),
        P("ptcl", None),
        P("ptcl"),
        P("cls", "ptcl", None),
        P("cls", "ptcl", None),
        P(),
    )
    out_specs = (P("ptcl", "cls"), P("cls", "ptcl", None))
    return jax.shard_map(local, mesh=mesh, in_specs=in_specs, out_specs=out_specs, check_vma=False)
```

profile of v0, /device:TPU:8, one launch (start us, length us, event | category | flops | bytes accessed | tf_op | source)
XLA Modules:
  0.0 491.1 jit_solution(3207926294490197985)
XLA Ops:
  7.2 0.0 copy-start
  7.2 0.8 broadcast_multiply_fusion.1
  8.0 0.8 copy.33
  8.8 0.1 eq.57
  8.9 0.1 eq.53
  9.1 0.1 copy.32
  9.2 0.1 mul.78
  9.4 0.6 reduce-window.6
  10.0 0.2 slice_reduce_fusion
  10.2 0.1 fusion.35
  10.3 1.4 scatter_custom_fusion.1
  11.7 1.4 scatter_custom_fusion
  13.2 3.5 gather_fusion
  16.6 0.7 all_to_all.36
  17.4 11.9 %all-to-all-start = ((bf16[64,1,8]{2,1,0:T(2,128)(2,1)}), bf16[64,1,8]{2,1,0:T(2,128)(2,1)S(1)}, u32[]{:S(2)}, u32[]{:S(2)}) async-start(bf16[64,1,8]{2,1,0:T(2,128)(2,1)} %all_to_all.36), calls=%async_computation | async-start | bytes 65536 | tf_op jit(solution)/shard_map/all_to_all | solution.py:53
  29.3 0.1 mul.82
  29.4 0.0 copy-done
  29.4 7.8 %gather_fusion.1 = bf16[512,8192]{1,0:T(8,128)(2,1)} fusion(bf16[128,8192]{1,0:T(8,128)(2,1)S(1)} %copy-done, s32[1024]{0:T(1024)S(1)} %pad_clamp_fusion), kind=kCustom, calls=%fused_computation.1 | custom fusion | bytes 16779264 | tf_op jit(solution)/shard_map/gather | solution.py:46
  37.2 7.2 %bitcast_multiply_fusion = bf16[64,8,8192]{2,1,0:T(8,128)(2,1)} fusion(bf16[512,8192]{1,0:T(8,128)(2,1)} %gather_fusion.1, bf16[64,8]{1,0:T(8,128)(2,1)S(1)} %mul.82), kind=kLoop, calls=%fused_computation.21 | loop fusion | flops 4194304 | bytes 16778240 | tf_op jit(solution)/shard_map/mul | solution.py:46
  44.5 0.0 all-to-all-done
  44.5 10.8 %all-to-all-start.1 = ((bf16[64,8,8192]{2,1,0:T(8,128)(2,1)}), bf16[64,8,8192]{2,1,0:T(8,128)(2,1)}, u32[]{:S(2)}, u32[]{:S(2)}) async-start(bf16[64,8,8192]{2,1,0:T(8,128)(2,1)} %bitcast_multiply_fusion), calls=%async_computation.1 | async-start | bytes 16777216 | tf_op jit(solution)/shard_map/all_to_all | solution.py:47
  55.2 5.1 %multiply_reduce_fusion = f32[512]{0:T(512)S(1)} fusion(bf16[1,512,8192]{2,1,0:T(8,128)(2,1)} %param.11), kind=kLoop, calls=%fused_computation.14 | loop fusion | flops 12582400 | bytes 8390656 | tf_op jit(solution)/shard_map/reduce_sum | solution.py:45
  60.4 0.1 convert_reduce_fusion
  60.5 0.1 reshape.117
  60.5 179.4 %all-to-all-done.1 = bf16[64,8,8192]{2,1,0:T(8,128)(2,1)} async-done(((bf16[64,8,8192]{2,1,0:T(8,128)(2,1)}), bf16[64,8,8192]{2,1,0:T(8,128)(2,1)}, u32[]{:S(2)}, u32[]{:S(2)}) %all-to-all-start.1) | async-done | bytes 8388640 | tf_op jit(solution)/shard_map/all_to_all | solution.py:47
  239.9 9.9 %fusion.44 = (f32[512]{0:T(512)S(1)}, f32[512,512]{1,0:T(8,128)S(1)}) fusion(f32[512]{0:T(512)S(1)} %broadcast_multiply_fusion, bf16[1,512,8192]{2,1,0:T(8,128)(2,1)} %param.11, bf16[64,8,8192]{2,1,0:T(8,128)(2,1)} %all-to-all-done.1, f32[512]{0:T(512)S(1)} %reshape.117), kind=kOutput, calls=%fused_computation.71 | convolution fusion | flops 4295753216 | bytes 17831936 | tf_op jit(solution)/shard_map/dot_general | solution.py:50
  249.8 0.7 all_to_all.32
  250.5 6.7 %all-to-all-start.3 = ((f32[64,1,8]{2,1,0:T(1,128)}), f32[64,1,8]{2,1,0:T(1,128)S(1)}, u32[]{:S(2)}, u32[]{:S(2)}) async-start(f32[64,1,8]{2,1,0:T(1,128)} %bitcast.9), calls=%async_computation.3 | async-start | bytes 65536 | tf_op jit(solution)/shard_map/all_to_all | solution.py:65
  257.2 0.3 exponential_reduce_fusion
  257.5 0.7 all_to_all.30
  258.2 8.4 %all-to-all-done.3 = f32[64,1,8]{2,1,0:T(1,128)S(1)} async-done(((f32[64,1,8]{2,1,0:T(1,128)}), f32[64,1,8]{2,1,0:T(1,128)S(1)}, u32[]{:S(2)}, u32[]{:S(2)}) %all-to-all-start.3) | async-done | bytes 2080 | tf_op jit(solution)/shard_map/all_to_all | solution.py:65
  266.7 4.5 all-to-all-start.2
  271.2 0.0 reduce-scatter.2.cloned.1.call-start
  271.2 0.5 broadcast.112
  271.8 0.7 reduce.12
  272.5 0.1 sub.65
  272.6 0.3 select_reduce_fusion.1
  272.9 7.9 %all-gather.2 = f32[4,1,128]{2,1,0:T(1,128)S(1)} all-gather(f32[1,1,128]{2,1,0:T(1,128)S(1)} %bitcast.98), channel_id=2, replica_groups=mesh['cls'=4,'ptcl'=64] {'cls'}, dimensions={0}, use_global_device_ids=true | all-gather | bytes 2560 | tf_op jit(solution)/shard_map/all_gather | solution.py:10
  280.7 0.0 all-to-all-done.2
  280.8 0.7 reduce.13
  281.5 0.1 mul.88
  281.6 0.4 select_reduce_fusion
  281.9 9.4 %all-gather.3 = f32[4,1,128]{2,1,0:T(1,128)S(1)} all-gather(f32[1,1,128]{2,1,0:T(1,128)S(1)} %bitcast.100), channel_id=3, replica_groups=mesh['cls'=4,'ptcl'=64] {'cls'}, dimensions={0}, use_global_device_ids=true | all-gather | bytes 2560 | tf_op jit(solution)/shard_map/all_gather | solution.py:10
  291.3 0.1 while.12
  291.5 0.5 multiply_bitcast_fusion
  292.0 3.3 gather_fusion.2
  295.4 0.1 all_to_all.34
  295.4 19.6 %all_to_all.42 = f32[64,1,8]{2,1,0:T(1,128)S(1)} all-to-all(f32[64,1,8]{2,1,0:T(1,128)S(1)} %bitcast.94), channel_id=1, replica_groups=mesh['cls'=4,'ptcl'=64] {'ptcl'}, dimensions={0} | all-to-all | bytes 4096 | tf_op jit(solution)/shard_map/all_to_all | solution.py:84
  315.1 0.1 copy.40
  315.1 0.0 copy-start.2
  315.1 24.9 %fusion.13 = bf16[64,64,8,128]{3,2,1,0:T(8,128)(2,1)S(1)} fusion(bf16[64,8,8192]{2,1,0:T(8,128)(2,1)} %all-to-all-done.1, f32[64,8,512]{2,1,0:T(8,128)S(1)} %bitcast.93, f32[64,8]{0,1:T(8,128)S(1)} %copy.40), kind=kOutput, calls=%fused_computation.24 | convolution fusion | flops 4299948032 | bytes 17827840 | tf_op jit(solution)/shard_map/dot_general | solution.py:86
  340.1 0.0 copy-done.2
  340.1 0.0 copy-start.1
  340.1 3.5 fusion.5
  343.6 0.0 copy-done.1
  343.6 3.5 fusion.45
  347.1 0.0 reduce-scatter.2.cloned.1.call-update
  347.2 137.1 %reduce-scatter.2.cloned.1.call-done = f32[128,128]{1,0:T(8,128)} async-done(((f32[8192,128]{1,0:T(8,128)}), f32[128,128]{1,0:T(8,128)}) %reduce-scatter.2.cloned.1.call-update) | async-done | bytes 65552 | tf_op jit(solution)/shard_map/reduce_scatter | solution.py:109
  (21 shorter events, 0.2 us)
Async XLA Ops:
  7.2 22.2 %copy-start = (bf16[128,8192]{1,0:T(8,128)(2,1)S(1)}, bf16[128,8192]{1,0:T(8,128)(2,1)}, u32[]{:S(2)}) copy-start(bf16[128,8192]{1,0:T(8,128)(2,1)} %param.8) | copy-start | bytes 6291460
  17.4 27.1 %all-to-all-start = ((bf16[64,1,8]{2,1,0:T(2,128)(2,1)}), bf16[64,1,8]{2,1,0:T(2,128)(2,1)S(1)}, u32[]{:S(2)}, u32[]{:S(2)}) async-start(bf16[64,1,8]{2,1,0:T(2,128)(2,1)} %all_to_all.36), calls=%async_computation | async-start | bytes 65536 | tf_op jit(solution)/shard_map/all_to_all | solution.py:53
  44.5 195.5 %all-to-all-start.1 = ((bf16[64,8,8192]{2,1,0:T(8,128)(2,1)}), bf16[64,8,8192]{2,1,0:T(8,128)(2,1)}, u32[]{:S(2)}, u32[]{:S(2)}) async-start(bf16[64,8,8192]{2,1,0:T(8,128)(2,1)} %bitcast_multiply_fusion), calls=%async_computation.1 | async-start | bytes 16777216 | tf_op jit(solution)/shard_map/all_to_all | solution.py:47
  250.5 16.1 %all-to-all-start.3 = ((f32[64,1,8]{2,1,0:T(1,128)}), f32[64,1,8]{2,1,0:T(1,128)S(1)}, u32[]{:S(2)}, u32[]{:S(2)}) async-start(f32[64,1,8]{2,1,0:T(1,128)} %bitcast.9), calls=%async_computation.3 | async-start | bytes 65536 | tf_op jit(solution)/shard_map/all_to_all | solution.py:65
  266.7 14.1 %all-to-all-start.2 = ((f32[64,1,8]{2,1,0:T(1,128)}), f32[64,1,8]{2,1,0:T(1,128)S(1)}, u32[]{:S(2)}, u32[]{:S(2)}) async-start(f32[64,1,8]{2,1,0:T(1,128)} %bitcast.8), calls=%async_computation.2 | async-start | bytes 65536 | tf_op jit(solution)/shard_map/all_to_all | solution.py:66
  271.2 213.1 %reduce-scatter.2.cloned.1.call-start = ((), (), s32[]{:S(2)}) async-start(), calls=%async_computation.6 | async-start | bytes 4259840 | tf_op jit(solution)/shard_map/reduce_scatter | solution.py:109
  315.1 24.9 %copy-start.2 = (s32[1,512,64]{1,2,0:T(8,128)S(1)}, s32[1,512,64]{1,2,0:T(8,128)}, u32[]{:S(2)}) copy-start(s32[1,512,64]{1,2,0:T(8,128)} %param.12) | copy-start | bytes 393220
  340.1 3.5 copy-start.1
Sparse Core Ops, SparseCore 0:
  347.3 136.9 reduce-scatter.1
where the time goes:
time: 492 us; the launch traced here: 491 us
  waiting for transfers between devices  325 us (66%)
  matrix products  41.8 us (8%)
  blocking collectives  36.9 us (8%)
  starting transfers between devices  33.9 us (7%)
  local copies, waits for them, and re-layouts  22.1 us (4%)
  other arithmetic  17 us (3%)
  between operations  14.3 us (3%)
    all_to_all x1, waiting for transfers between devices, local(): lax.all_to_all(send_rows, 'ptcl', split_axis=0, concat_axis=0, tiled=True)  179 us
    reduce_scatter x1, waiting for transfers between devices, local(): lax.psum_scatter(partial_volume, 'ptcl', scatter_dimension=0, tiled=True)  137 us
    dot_general x1, matrix products, local(): lax.dot_general(weights.reshape(-1, per_bin), got_rows.reshape(-1, pixels...  24.9 us
    all_to_all x1, blocking collectives, local(): lax.all_to_all(slot_log, 'ptcl', split_axis=0, concat_axis=0, tiled=True)  19.6 us
    all_gather x2, blocking collectives, joined(): pieces = jax.tree.map(lambda part: lax.all_gather(part, axis), value)  17.3 us
    all_to_all x1, starting transfers between devices, local(): lax.all_to_all(send_scale, 'ptcl', split_axis=0, concat_axis=0, tiled=True)  11.9 us
    all_to_all x1, starting transfers between devices, local(): lax.all_to_all(send_rows, 'ptcl', split_axis=0, concat_axis=0, tiled=True)  10.8 us
    dot_general x1, matrix products, local(): lax.dot_general(pixel_rows, ref_rows, (((1,), (1,)), ((), ())), preferred...  9.89 us
  transfers between devices with their start and end apart: 5, of which 3 were waited for; matrix products, arithmetic and copies ran while one was open for 5% of the time, Pallas kernels for 0%

commit v1 on v0

v1 whole, which is shorter than its diff:
```python
import functools

import jax
import jax.numpy as jnp
from jax import lax
from jax.experimental import pallas as pl
from jax.experimental.pallas import tpu as pltpu
from jax.sharding import PartitionSpec as P

MESH = pl.DeviceIdType.MESH
F32, BF16, I32 = jnp.float32, jnp.bfloat16, jnp.int32
NZ = 8
CW = 256
LINE = 128
SLOTS = 8


def iota(shape, dim):
    return lax.broadcasted_iota(I32, shape, dim)


def dot(a, b, ca=1, cb=0):
    return lax.dot_general(a, b, (((ca,), (cb,)), ((), ())), preferred_element_type=F32)


def thirds(v):
    hi = v.astype(BF16)
    rest = v - hi.astype(F32)
    mid = rest.astype(BF16)
    low = (rest - mid.astype(F32)).astype(BF16)
    return hi, mid, low


def kernel(ny, nx, nz, nch, img_hbm, meta_ref, refs_hbm, idx_ref, interp_hbm, prob_ref, vol_ref,
           img, meta, g, g2, sendbuf, recv, xs_all, refs, onehot, interp, score, weight, hnorm,
           psend, ptab, stat, bsend, btab, csend, ctab, vb, sib, xs, xr, zs, zr,
           load_sem, ex_ss, ex_rs, a_ss, a_rs, a_loc, p_ss, p_rs, k_ss, k_rs, k_loc,
           y_ss, y_rs, f_ss, f_rs, s_ss, s_rs, b_ss, b_rs, c_ss, c_rs,
           v_ss, v_rs, x_ss, x_rs, z_ss, z_rs):
    nq = nx * nz
    y, d = lax.axis_index("cls"), lax.axis_index("ptcl")
    q, k = d // 2, d % 2
    x, z = q // nz, q % nz
    other = 1 - k
    part = meta_ref.shape[1]
    span = nch * CW
    n_ref = refs.shape[0]
    rows = nq * 16
    nw = rows // 128
    sibling = (y, q * 2 + other)
    y_up, y_dn = (y + 1) % ny, (y + ny - 1) % ny
    up, dn = (y_up, d), (y_dn, d)

    def remote(src, dst, ss, rs, dev):
        return pltpu.make_async_remote_copy(src_ref=src, dst_ref=dst, send_sem=ss, recv_sem=rs,
                                            device_id=dev, device_id_type=MESH)

    ld_img = pltpu.make_async_copy(
        img_hbm.at[:, pl.ds(pl.multiple_of((y * 2 + k) * span, span), span)], img.at[k], load_sem.at[0])
    ld_refs = pltpu.make_async_copy(refs_hbm, refs, load_sem.at[1])
    ld_int = pltpu.make_async_copy(interp_hbm, interp, load_sem.at[2])
    ld_img.start()
    ld_refs.start()
    ld_int.start()

    bar = pltpu.get_barrier_semaphore()

    def greet(i, c):
        q2 = (q + i) % nq
        pl.semaphore_signal(bar, inc=1, device_id=(y, q2 * 2 + k), device_id_type=MESH)
        return c

    lax.fori_loop(1, nq, greet, 0)

    def greet_col(i, c):
        c2 = (y * 2 + k + i) % (2 * ny)
        pl.semaphore_signal(bar, inc=1, device_id=(c2 // 2, q * 2 + c2 % 2), device_id_type=MESH)
        return c

    lax.fori_loop(1, 2 * ny, greet_col, 0)
    pl.semaphore_wait(bar, nq - 1 + 2 * ny - 1)

    ex_meta = remote(meta_ref, meta.at[k], ex_ss.at[0], ex_rs.at[0], sibling)
    ex_meta.start()
    ex_img = remote(img_hbm.at[:, pl.ds(pl.multiple_of((y * 2 + other) * span, span), span)], img.at[k],
                    ex_ss.at[1], ex_rs.at[1], sibling)
    ex_img.start()
    meta[k] = meta_ref[...]
    ex_meta.wait_recv()

    both = meta[...]
    n_bin, pairs = nq * 2, 2 * part
    before = (iota((pairs, pairs), 0) < iota((pairs, pairs), 1)).astype(F32).astype(BF16)
    r = iota((2 * rows, n_bin), 0)
    row_bin = (lax.shift_right_logical(r, 4) % nq) * 2 + lax.shift_right_logical(r, 4) // nq
    expand = (row_bin == iota((2 * rows, n_bin), 1)).astype(F32).astype(BF16)
    r2 = iota((2 * rows, pairs), 0)
    folded = []
    for k2 in range(2):
        bins = jnp.concatenate([both[k2, 0:1], both[k2, 1:2]], axis=1)
        named = (iota((n_bin, pairs), 0).astype(F32) == bins).astype(F32)
        rank = dot(named.astype(BF16), before)
        marked = (named * (rank + 1.0)).astype(BF16)
        spread = dot(expand, marked)
        want = jnp.where((lax.shift_right_logical(r2, 3) & 1) == k2, (r2 & 7) + 1, -1).astype(F32)
        hit = (spread == want).astype(F32)
        g2[:, :, k2 * pairs:(k2 + 1) * pairs] = hit.astype(BF16).reshape(2, rows, pairs)
        folded.append(hit[:, :part] + hit[:, part:])
    g[...] = jnp.concatenate(folded, axis=1).astype(BF16)

    ld_img.wait()
    ex_img.wait_recv()
    for j in range(nch):
        cols = slice(j * CW, (j + 1) * CW)
        pix = jnp.concatenate([img[0, :, cols], img[1, :, cols]], axis=0)
        sendbuf[j] = dot(g[...], pix).astype(BF16).reshape(2, nq, 16, CW)

        def send(i, c):
            q2 = (q + i) % nq
            remote(sendbuf.at[j, :, q2], recv.at[j, :, q], a_ss.at[j], a_rs.at[j], (y, q2 * 2 + k)).start()
            return c

        lax.fori_loop(1, nq, send, 0)
        pltpu.make_async_copy(sendbuf.at[j, :, q], recv.at[j, :, q], a_loc.at[j]).start()

    def scatter(src, dst, ss, rs):
        def one(i, c):
            q2 = (q + i) % nq
            remote(src.at[q2 // 8], dst.at[q], ss, rs, (y, q2 * 2 + k)).start()
            return c

        lax.fori_loop(1, nq, one, 0)
        dst[q] = src[q // 8]

    def gathered(dst, ss, rs):
        remote(dst.at[pl.ds(0, nq - 1)], dst.at[pl.ds(0, nq - 1)], ss, rs, sibling).wait_recv()

    def sent(dst, ss, rs):
        remote(dst.at[pl.ds(0, nq - 1)], dst.at[pl.ds(0, nq - 1)], ss, rs, sibling).wait_send()

    def windows(dst, value):
        for w in range(nw):
            dst[w] = value[:, w * 128:(w + 1) * 128]

    def unpack(tab):
        t = tab[...]
        lane = iota(t.shape, 2)
        t = jnp.where(lax.shift_right_logical(lane, 4) == q % 8, t, 0.0)
        t = t.reshape(nq * 8, 128)
        for s in (64, 32, 16):
            t = t + pltpu.roll(t, s, 1)
        t = jnp.concatenate([t] * nw, axis=1).reshape(nq, 8, rows)
        keep = lax.shift_right_logical(iota(t.shape, 2), 4) == iota(t.shape, 0)
        return jnp.sum(jnp.where(keep, t, 0.0), axis=0)

    prec = jnp.concatenate([both[0, 2:3], both[0, 2:3], both[1, 2:3], both[1, 2:3]], axis=1)
    prec = jnp.broadcast_to(prec, (8, 2 * pairs)).astype(BF16)
    windows(psend, dot(prec, g2[k], 1, 1))
    scatter(psend, ptab, p_ss, p_rs)

    ld_refs.wait()
    hnorm[...] = jnp.zeros_like(hnorm)

    def norm(i, c):
        v = refs[:, pl.ds(pl.multiple_of(i * 128, 128), 128)].astype(F32)
        hnorm[...] += v * v
        return c

    lax.fori_loop(0, refs.shape[1] // 128, norm, 0)
    half = 0.5 * jnp.sum(hnorm[...], axis=1, keepdims=True)

    def bands(i, c):
        onehot[i] = (iota((LINE, n_ref), 0) == idx_ref[pl.ds(i, 1), :]).astype(F32).astype(BF16)
        return c

    lax.fori_loop(0, onehot.shape[0], bands, 0)
    score[...] = jnp.zeros_like(score)

    def piece(yy, k2, j):
        return (yy * 2 + k2) * nch + j

    def add_score(p):
        r_p = refs[:, pl.ds(pl.multiple_of(p * CW, CW), CW)]
        score[...] += dot(r_p, xs_all[p].reshape(rows, CW), 1, 1)

    def y_copy(src, p, way, k2, j):
        return remote(src, xs_all.at[p], y_ss.at[way, k2, j], y_rs.at[way, k2, j], up if way == 0 else dn)

    def y_wait(yy, way, k2, j):
        p = piece(yy, k2, j)
        remote(xs_all.at[p], xs_all.at[p], y_ss.at[way, k2, j], y_rs.at[way, k2, j], up).wait_recv()

    def f_copy(p, way, j):
        return remote(xs_all.at[p], xs_all.at[p], f_ss.at[way, j], f_rs.at[way, j], up if way == 0 else dn)

    def chunk_wait(j):
        remote(recv.at[j, :, pl.ds(0, nq - 1)], recv.at[j, :, pl.ds(0, nq - 1)], a_ss.at[j], a_rs.at[j],
               sibling).wait_recv()
        pltpu.make_async_copy(sendbuf.at[j, :, q], recv.at[j, :, q], a_loc.at[j]).wait()

    def own_copy(j):
        return pltpu.make_async_copy(recv.at[j, k], xs_all.at[piece(y, k, j)], k_loc.at[j])

    def sib_copy(j):
        return remote(recv.at[j, other], xs_all.at[piece(y, k, j)], k_ss.at[j], k_rs.at[j], sibling)

    def stage0(j):
        chunk_wait(j)
        sib_copy(j).start()
        for way in range(2):
            y_copy(recv.at[j, k], piece(y, k, j), way, k, j).start()
        own_copy(j).start()
        sib_copy(j).wait_recv()
        for way in range(2):
            y_copy(xs_all.at[piece(y, other, j)], piece(y, other, j), way, other, j).start()
        own_copy(j).wait()

    def stage1(j):
        y_wait(y_dn, 0, 0, j)
        f_copy(piece(y_dn, 0, j), 0, j).start()
        y_wait(y_up, 1, 1, j)
        f_copy(piece(y_up, 1, j), 1, j).start()
        add_score(piece(y, 0, j))
        add_score(piece(y, 1, j))
        add_score(piece(y_dn, 0, j))
        add_score(piece(y_up, 1, j))
        y_wait(y_dn, 0, 1, j)
        y_wait(y_up, 1, 0, j)
        add_score(piece(y_dn, 1, j))
        add_score(piece(y_up, 0, j))

    def stage2(j):
        far = (y + 2) % ny
        for way in range(2):
            f_copy(piece(far, way, j), way, j).wait_recv()
            add_score(piece(far, way, j))

    for j in range(nch + 2):
        if j < nch:
            stage0(j)
        if 1 <= j <= nch:
            stage1(j - 1)
        if j >= 2:
            stage2(j - 2)

    gathered(ptab, p_ss, p_rs)
    scale = unpack(ptab)[0:1]
    s = scale * (score[...] - half)
    score[...] = s
    top = jnp.max(s, axis=0, keepdims=True)
    total = jnp.sum(jnp.exp(s - top), axis=0, keepdims=True)
    col = y * 2 + k
    stat[col] = jnp.concatenate([top, total], axis=0)

    def share(i, c):
        c2 = (col + i) % (2 * ny)
        remote(stat.at[col], stat.at[col], s_ss, s_rs, (c2 // 2, q * 2 + c2 % 2)).start()
        return c

    lax.fori_loop(1, 2 * ny, share, 0)
    all_stat = stat.at[pl.ds(0, 2 * ny - 1)]
    remote(all_stat, all_stat, s_ss, s_rs, sibling).wait_recv()
    line = [[], [], []]
    for kb in range(2):
        tops = [stat[2 * yy + kb, 0:1] for yy in range(ny)]
        high = functools.reduce(jnp.maximum, tops)
        mass = sum(stat[2 * yy + kb, 1:2] * jnp.exp(tops[yy] - high) for yy in range(ny))
        mine = stat[2 * y + kb]
        line[0].append(high)
        line[1].append(mass)
        line[2].append(mine[1:2] * jnp.exp(mine[0:1] - high))
    table = jnp.concatenate(line[0] + line[1] + line[2] + [jnp.zeros((2, rows), F32)], axis=0)
    windows(bsend, table)
    scatter(bsend, btab, b_ss, b_rs)

    gathered(btab, b_ss, b_rs)
    cut = jnp.concatenate(thirds(unpack(btab)), axis=0)
    per_pair = []
    for kb in range(2):
        t = dot(cut, g2[kb])
        per_pair.append((t[16:24] + t[8:16]) + t[0:8])
    highs = per_pair[0][0:1] + per_pair[1][1:2]
    masses = per_pair[0][2:3] + per_pair[1][3:4]
    own = per_pair[0][4:5] + per_pair[1][5:6]
    logs, probs = [], []
    for k2 in range(2):
        lo, mi, hi = k2 * pairs, k2 * pairs + part, (k2 + 1) * pairs
        m0, m1 = highs[:, lo:mi], highs[:, mi:hi]
        high = jnp.maximum(m0, m1)
        log = high + jnp.log(masses[:, lo:mi] * jnp.exp(m0 - high) + masses[:, mi:hi] * jnp.exp(m1 - high))
        probs.append(own[:, lo:mi] * jnp.exp(m0 - log) + own[:, mi:hi] * jnp.exp(m1 - log))
        logs += [log, log]
    prob_ref[...] = jnp.where(k == 0, probs[0], probs[1])
    cut = jnp.concatenate(thirds(jnp.concatenate(logs, axis=1)) + (jnp.zeros((5, 2 * pairs), BF16),), axis=0)
    t = dot(cut, g2[k], 1, 1)
    slot_log = (t[2:3] + t[1:2]) + t[0:1]
    windows(csend, jnp.broadcast_to(slot_log, (8, rows)))
    scatter(csend, ctab, c_ss, c_rs)
    gathered(ctab, c_ss, c_rs)
    slot_log = unpack(ctab)[0:1]
    weight[...] = (n_ref * jnp.exp(score[...] - slot_log)).astype(BF16)

    ld_int.wait()

    def sib_send(t):
        return remote(vb.at[t, :, other], sib.at[t], v_ss.at[t], v_rs.at[t], sibling)

    def x_send(t, i):
        x2 = (x + nx - 1 - i) % nx
        return remote(xs.at[t, i], xr.at[t, i], x_ss.at[t], x_rs.at[t], (y, (x2 * nz + z) * 2 + k))

    def x_all(t):
        ref = xr.at[t]
        return remote(ref, ref, x_ss.at[t], x_rs.at[t], sibling)

    def z_send(t):
        z2 = (z + nz - 1 - t) % nz
        return remote(zs.at[t], zr.at[t], z_ss.at[t], z_rs.at[t], (y, (x * nz + z2) * 2 + k))

    def insert(t, i):
        q2 = ((x + nx - 1 - i) % nx) * nz + (z + nz - 1 - t) % nz
        image = dot(weight[...], xs_all[q2].reshape(rows, CW)).astype(BF16)
        for h in range(2):
            band = dot(onehot[2 * q2 + h], image[:, h * LINE:(h + 1) * LINE])
            hi = band.astype(BF16)
            low = (band - hi.astype(F32)).astype(BF16)
            block = interp[2 * q2 + h]
            vb[t, i, h] = dot(jnp.concatenate([hi, low], axis=1), jnp.concatenate([block, block], axis=0))

    def step(t, c):
        @pl.when(t < nz)
        def _():
            lax.fori_loop(0, nx, lambda i, c: (insert(t, i), c)[1], 0)
            sib_send(t).start()

        @pl.when((t >= 1) & (t <= nz))
        def _():
            u = t - 1
            sib_send(u).wait_recv()

            def one(i, c):
                xs[u, i] = (vb[u, i, k] + sib[u, i]).astype(BF16)
                x_send(u, i).start()
                return c

            lax.fori_loop(0, nx - 1, one, 0)

        @pl.when(t >= 2)
        def _():
            u = t - 2
            x_all(u).wait_recv()
            total = vb[u, nx - 1, k] + sib[u, nx - 1]
            for i in range(nx - 1):
                total += xr[u, i].astype(F32)

            @pl.when(u < nz - 1)
            def _():
                zs[u] = total.astype(BF16)
                z_send(u).start()

            @pl.when(u == nz - 1)
            def _():
                vol_ref[...] = total

        return c

    lax.fori_loop(0, nz + 2, step, 0)

    def z_add(t, c):
        z_send(t).wait_recv()
        vol_ref[...] += zr[t].astype(F32)
        return c

    lax.fori_loop(0, nz - 1, z_add, 0)

    ex_meta.wait_send()
    ex_img.wait_send()
    sent(ptab, p_ss, p_rs)
    remote(all_stat, all_stat, s_ss, s_rs, sibling).wait_send()
    sent(btab, b_ss, b_rs)
    sent(ctab, c_ss, c_rs)
    for j in range(nch):
        ref = recv.at[j, :, pl.ds(0, nq - 1)]
        remote(ref, ref, a_ss.at[j], a_rs.at[j], sibling).wait_send()
        sib_copy(j).wait_send()
        for way in range(2):
            y_copy(recv.at[j, k], piece(y, k, j), way, k, j).wait_send()
            y_copy(xs_all.at[piece(y, other, j)], piece(y, other, j), way, other, j).wait_send()
        f_copy(piece(y_dn, 0, j), 0, j).wait_send()
        f_copy(piece(y_up, 1, j), 1, j).wait_send()

    def v_done(t, c):
        sib_send(t).wait_send()
        x_all(t).wait_send()
        return c

    lax.fori_loop(0, nz, v_done, 0)
    lax.fori_loop(0, nz - 1, lambda t, c: (z_send(t).wait_send(), c)[1], 0)


def local(nz, images, bin_lists, precision, references, line_index, interp_blocks):
    ny, n_ptcl = lax.axis_size("cls"), lax.axis_size("ptcl")
    nq = n_ptcl // 2
    nx = nq // nz
    part, pixels = images.shape
    n_ref = references.shape[1]
    n_line = interp_blocks.shape[0]
    nch = pixels // (2 * ny * CW)
    rows = nq * 16
    nw = rows // 128
    meta = jnp.concatenate([bin_lists.T.astype(F32), precision.astype(F32)[None], jnp.zeros((5, part), F32)], axis=0)
    vmem, dma = pltpu.VMEM, pltpu.SemaphoreType.DMA
    whole = pl.BlockSpec(memory_space=pltpu.VMEM)
    far = pl.BlockSpec(memory_space=pl.ANY)
    flops = 4 * n_ref * rows * pixels
    prob, volume = pl.pallas_call(
        functools.partial(kernel, ny, nx, nz, nch),
        out_shape=(jax.ShapeDtypeStruct((1, part), F32), jax.ShapeDtypeStruct((LINE, LINE), F32)),
        in_specs=[far, whole, far, whole, far],
        out_specs=(whole, whole),
        scratch_shapes=[
            vmem((2, part, nch * CW), BF16),
            vmem((2, 8, part), F32),
            vmem((2 * rows, 2 * part), BF16),
            vmem((2, rows, 4 * part), BF16),
            vmem((nch, 2, nq, 16, CW), BF16),
            vmem((nch, 2, nq, 16, CW), BF16),
            vmem((2 * ny * nch, nq, 16, CW), BF16),
            vmem((n_ref, pixels), BF16),
            vmem((n_line, LINE, n_ref), BF16),
            vmem((n_line, LINE, LINE), BF16),
            vmem((n_ref, rows), F32),
            vmem((n_ref, rows), BF16),
            vmem((n_ref, 128), F32),
            vmem((nw, 8, 128), F32), vmem((nq, 8, 128), F32),
            vmem((2 * ny, 2, rows), F32),
            vmem((nw, 8, 128), F32), vmem((nq, 8, 128), F32),
            vmem((nw, 8, 128), F32), vmem((nq, 8, 128), F32),
            vmem((nz, nx, 2, LINE, LINE), F32),
            vmem((nz, nx, LINE, LINE), F32),
            vmem((nz, nx - 1, LINE, LINE), BF16), vmem((nz, nx - 1, LINE, LINE), BF16),
            vmem((nz - 1, LINE, LINE), BF16), vmem((nz - 1, LINE, LINE), BF16),
            dma((3,)), dma((2,)), dma((2,)),
            dma((nch,)), dma((nch,)), dma((nch,)),
            dma(()), dma(()),
            dma((nch,)), dma((nch,)), dma((nch,)),
            dma((2, 2, nch)), dma((2, 2, nch)),
            dma((2, nch)), dma((2, nch)),
            dma(()), dma(()), dma(()), dma(()), dma(()), dma(()),
            dma((nz,)), dma((nz,)), dma((nz,)), dma((nz,)), dma((nz - 1,)), dma((nz - 1,)),
        ],
        compiler_params=pltpu.CompilerParams(collective_id=0, has_side_effects=True, vmem_limit_bytes=58 << 20),
        cost_estimate=pl.CostEstimate(flops=flops, bytes_accessed=n_ref * pixels * 2, transcendentals=0),
    )(images, meta, references[0], line_index[0].T, interp_blocks)
    return prob.reshape(part, 1), volume[None]


def solution(mesh, nz=NZ):
    in_specs = (
        P("ptcl", None),
        P("ptcl", None),
        P("ptcl"),
        P("cls", "ptcl", None),
        P("cls", "ptcl", None),
        P(),
    )
    out_specs = (P("ptcl", "cls"), P("cls", "ptcl", None))
    return jax.shard_map(functools.partial(local, nz), mesh=mesh, in_specs=in_specs, out_specs=out_specs,
                         check_vma=False)
```

time: 492 us -> 162 us (0.33)
  waiting for transfers between devices: 325 us -> 0 us
  Pallas kernels: 0 us -> 156 us
  matrix products: 41.8 us -> 0 us
  blocking collectives: 36.9 us -> 0 us
  starting transfers between devices: 33.9 us -> 0 us
  local copies, waits for them, and re-layouts: 22.1 us -> 2.67 us
  other arithmetic: 17 us -> 2 us
  between operations: 14.3 us -> 0.64 us
    all_to_all x4 -> x0, waiting for transfers between devices: 188 us -> none  [the longest x1 179 us: local(): lax.all_to_all(send_rows, 'ptcl', split_axis=0, concat_axis=0, tiled=True)]
    pallas_call x0 -> x1, Pallas kernels: none -> 156 us  [local(): pl.pallas_call(functools.partial(kernel, ny, nx, nz, nch), out_shape=(jax...]
    reduce_scatter x1 -> x0, waiting for transfers between devices: 137 us -> none  [local(): lax.psum_scatter(partial_volume, 'ptcl', scatter_dimension=0, tiled=True)]
    dot_general x4 -> x0, matrix products: 41.8 us -> none  [the longest x1 24.9 us: local(): lax.dot_general(weights.reshape(-1, per_bin), got_rows.reshape(-1, pixels...]
    all_to_all x4 -> x0, starting transfers between devices: 33.9 us -> none  [the longest x1 11.9 us: local(): lax.all_to_all(send_scale, 'ptcl', split_axis=0, concat_axis=0, tiled=True)]
    all_to_all x1 -> x0, blocking collectives: 19.6 us -> none  [local(): lax.all_to_all(slot_log, 'ptcl', split_axis=0, concat_axis=0, tiled=True)]
    all_gather x2 -> x0, blocking collectives: 17.3 us -> none  [joined(): pieces = jax.tree.map(lambda part: lax.all_gather(part, axis), value)]
    gather x3 -> x0, local copies, waits for them, and re-layouts: 14.6 us -> none  [the longest x1 7.83 us: local(): images[slot_src] * occupied[:, None]]
  transfers between devices with their start and end apart: 5 -> 0, of which waited for: 3 -> 0; matrix products, arithmetic and copies ran while one was open for 5% -> 0% of each run, Pallas kernels for 0% -> 0%
where the time goes in v1:
time: 162 us; the launch traced here: 161 us
  Pallas kernels  156 us (96%)
  local copies, waits for them, and re-layouts  2.67 us (2%)
  other arithmetic  2 us (1%)
    pallas_call x1, Pallas kernels, local(): pl.pallas_call(functools.partial(kernel, ny, nx, nz, nch), out_shape=(jax...  156 us

profile of v1, /device:TPU:8, one launch (start us, length us, event | category | flops | bytes accessed | tf_op | source)
XLA Modules:
  0.0 161.5 jit_solution(5927724067793779260)
XLA Ops:
  0.6 0.7 bitcast_convert_fusion
  1.3 0.1 pad.2.clone
  1.4 0.7 convert_bitcast_fusion
  2.0 0.7 maximum_maximum_fusion.meta_ref
  2.7 156.1 %shard_map.77 = (f32[1,128]{1,0:T(1,128)}, f32[128,128]{1,0:T(8,128)}) custom-call(bf16[128,8192]{1,0:T(8,128)(2,1)} %img_hbm.1, f32[8,128]{1,0:T(8,128)} %maximum_maximum_fusion.meta_ref, bf16[512,8192]{1,0:T(8,128)(2,1)} %bitcast.12, s32[64,512]{1,0:T(8,128)} %bitcast.13, bf16[64,128,128]{2,1,0:T(8,128)(2,1)} %interp_hbm.1), custom_call_target="tpu_custom_call" | custom-call | flops 8589934592 | bytes 8388608 | tf_op jit(solution)/shard_map/pallas_call | solution.py:416
  158.9 1.1 copy.10
  160.0 1.5 copy.11
  (1 shorter events, 0.0 us)

commit v2 on v1

v2 whole, which is shorter than its diff:
```python
import functools

import jax
import jax.numpy as jnp
from jax import lax
from jax.experimental import pallas as pl
from jax.experimental.pallas import tpu as pltpu
from jax.sharding import PartitionSpec as P

MESH = pl.DeviceIdType.MESH
F32, BF16, I32 = jnp.float32, jnp.bfloat16, jnp.int32
NZ = 8
CW = 128
FAR = 2
LINE = 128
SLOTS = 8


def iota(shape, dim):
    return lax.broadcasted_iota(I32, shape, dim)


def dot(a, b, ca=1, cb=0):
    return lax.dot_general(a, b, (((ca,), (cb,)), ((), ())), preferred_element_type=F32)


def thirds(v):
    hi = v.astype(BF16)
    rest = v - hi.astype(F32)
    mid = rest.astype(BF16)
    low = (rest - mid.astype(F32)).astype(BF16)
    return hi, mid, low


def kernel(ny, nx, nz, nch, far_n, img_hbm, bins_ref, prec_ref, refs_hbm, idx_ref, interp_hbm, prob_ref, vol_ref,
           img, meta, g, g2, sendbuf, recv, xs_all, refs, onehot, interp, score, weight, hnorm,
           psend, ptab, stat, lrow, ltab, dsend, dtab, vb, sib, xs, xr, zs, zr,
           load_sem, ex_ss, ex_rs, a_ss, a_rs, a_loc, p_ss, p_rs, k_ss, k_rs, k_loc,
           y_ss, y_rs, f_ss, f_rs, s_ss, s_rs, b_ss, b_rs, d_ss, d_rs,
           v_ss, v_rs, x_ss, x_rs, z_ss, z_rs):
    nq = nx * nz
    y, d = lax.axis_index("cls"), lax.axis_index("ptcl")
    q, k = d // 2, d % 2
    x, z = q // nz, q % nz
    other = 1 - k
    part = bins_ref.shape[1]
    n_bin, pairs = nq * 2, 2 * part
    n_chunk = nch + far_n
    n_ref = refs.shape[0]
    rows = nq * 16
    nw = rows // 128
    sibling = (y, q * 2 + other)
    y_up, y_dn, y_far = (y + 1) % ny, (y + ny - 1) % ny, (y + 2) % ny
    up, dn = (y_up, d), (y_dn, d)

    def remote(src, dst, ss, rs, dev):
        return pltpu.make_async_remote_copy(src_ref=src, dst_ref=dst, send_sem=ss, recv_sem=rs,
                                            device_id=dev, device_id_type=MESH)

    def piece(yy, k2, j):
        return (yy * 2 + k2) * nch + j

    def pixels(p, count):
        return pl.ds(pl.multiple_of(p * CW, CW), count * CW)

    def plane(i):
        return (y, ((q + i) % nq) * 2 + k)

    bar = pltpu.get_barrier_semaphore()

    def greet(i, c):
        pl.semaphore_signal(bar, inc=1, device_id=(y, (d + i) % n_bin), device_id_type=MESH)
        return c

    def greet_y(i, c):
        pl.semaphore_signal(bar, inc=1, device_id=((y + i) % ny, d), device_id_type=MESH)
        return c

    lax.fori_loop(1, n_bin, greet, 0)
    lax.fori_loop(1, ny, greet_y, 0)

    def img_parts(core):
        return ((img_hbm.at[:, pixels(piece(y, core, 0), nch)], img.at[k, :, pl.ds(0, nch * CW)]),
                (img_hbm.at[:, pixels(piece(y_far, core, nch - far_n), far_n)],
                 img.at[k, :, pl.ds(nch * CW, far_n * CW)]))

    ld_img = [pltpu.make_async_copy(a, b, load_sem.at[i]) for i, (a, b) in enumerate(img_parts(k))]
    ld_refs = pltpu.make_async_copy(refs_hbm, refs, load_sem.at[2])
    ld_int = pltpu.make_async_copy(interp_hbm, interp, load_sem.at[3])
    for ld in ld_img + [ld_refs, ld_int]:
        ld.start()
    meta[k, 0:2] = bins_ref[...].astype(F32)
    meta[k, 2:3] = prec_ref[...].astype(F32)
    meta[k, 3:8] = jnp.zeros((5, part), F32)
    before = (iota((pairs, pairs), 0) < iota((pairs, pairs), 1)).astype(F32).astype(BF16)
    r = iota((2 * rows, n_bin), 0)
    row_bin = (lax.shift_right_logical(r, 4) % nq) * 2 + lax.shift_right_logical(r, 4) // nq
    expand = (row_bin == iota((2 * rows, n_bin), 1)).astype(F32).astype(BF16)
    pl.semaphore_wait(bar, n_bin - 1 + ny - 1)

    ex = [remote(meta.at[k], meta.at[k], ex_ss.at[0], ex_rs.at[0], sibling)]
    ex += [remote(a, b, ex_ss.at[1 + i], ex_rs.at[1 + i], sibling) for i, (a, b) in enumerate(img_parts(other))]
    for e in ex:
        e.start()
    ex[0].wait_recv()

    both = meta[...]
    r2 = iota((2 * rows, pairs), 0)
    folded, mates, mate_ranks, precs = [], [], [], []
    for k2 in range(2):
        bins = jnp.concatenate([both[k2, 0:1], both[k2, 1:2]], axis=1)
        named = (iota((n_bin, pairs), 0).astype(F32) == bins).astype(F32)
        rank = named * dot(named.astype(BF16), before)
        spread = dot(expand, (named + rank).astype(BF16))
        want = jnp.where((lax.shift_right_logical(r2, 3) & 1) == k2, (r2 & 7) + 1, -1).astype(F32)
        hit = (spread == want).astype(F32)
        g2[:, :, k2 * pairs:(k2 + 1) * pairs] = hit.astype(BF16).reshape(2, rows, pairs)
        folded.append(hit[:, :part] + hit[:, part:])
        ranks = jnp.sum(rank, axis=0, keepdims=True)
        mates += [both[k2, 1:2], both[k2, 0:1]]
        mate_ranks += [ranks[:, part:], ranks[:, :part]]
        precs += [both[k2, 2:3]] * 2
    g[...] = jnp.concatenate(folded, axis=1).astype(BF16)

    def send_chunks(j, n):
        cols = slice(j * CW, (j + n) * CW)
        pix = jnp.concatenate([img[0, :, cols], img[1, :, cols]], axis=0)
        out = dot(g[...], pix).astype(BF16)
        for m in range(n):
            sendbuf[j + m] = out[:, m * CW:(m + 1) * CW].reshape(2, nq, 16, CW)

            def send(i, c):
                remote(sendbuf.at[j + m, :, (q + i) % nq], recv.at[j + m, :, q], a_ss.at[j + m], a_rs.at[j + m],
                       plane(i)).start()
                return c

            lax.fori_loop(1, nq, send, 0)
            pltpu.make_async_copy(sendbuf.at[j + m, :, q], recv.at[j + m, :, q], a_loc.at[j + m]).start()

    ld_img[0].wait()
    ex[1].wait_recv()
    for j in range(0, nch, 2):
        send_chunks(j, min(2, nch - j))
    ld_img[1].wait()
    ex[2].wait_recv()
    for j in range(nch, n_chunk, 2):
        send_chunks(j, min(2, n_chunk - j))

    def windows(dst, value):
        for w in range(nw):
            dst[w] = value[:, w * 128:(w + 1) * 128]

    def own_lanes(t):
        axis = t.ndim - 1
        t = jnp.where(lax.shift_right_logical(iota(t.shape, axis), 4) == q % 8, t, 0.0)
        for s in (64, 32, 16):
            t = t + pltpu.roll(t, s, axis)
        return t

    def by_chip(t):
        n = t.shape[1]
        t = t.reshape(nw, 8, n, 128)
        t = jnp.sum(jnp.where(lax.shift_right_logical(iota(t.shape, 3), 4) == iota(t.shape, 1), t, 0.0), axis=1)
        return jnp.concatenate([t[w] for w in range(nw)], axis=1)

    facts = [jnp.concatenate(v, axis=1) for v in (precs, mates, mate_ranks)]
    facts = jnp.concatenate(facts + [jnp.zeros((5, 2 * pairs), F32)], axis=0).astype(BF16)
    windows(psend, dot(facts, g2[k], 1, 1))

    def send_facts(i, c):
        remote(psend.at[((q + i) % nq) // 8], ptab.at[q], p_ss, p_rs, plane(i)).start()
        return c

    lax.fori_loop(1, nq, send_facts, 0)
    ptab[q] = psend[q // 8]
    facts_done = remote(ptab.at[pl.ds(0, nq - 1)], ptab.at[pl.ds(0, nq - 1)], p_ss, p_rs, sibling)

    ld_refs.wait()
    hnorm[...] = jnp.zeros_like(hnorm)

    def norm(i, c):
        v = refs[:, pl.ds(pl.multiple_of(i * 128, 128), 128)].astype(F32)
        hnorm[...] += v * v
        return c

    lax.fori_loop(0, refs.shape[1] // 128, norm, 0)

    def bands(i, c):
        onehot[i] = (iota((LINE, n_ref), 0) == idx_ref[pl.ds(i, 1), :]).astype(F32).astype(BF16)
        return c

    lax.fori_loop(0, onehot.shape[0], bands, 0)
    score[...] = jnp.zeros_like(score)

    def slab(p):
        return jnp.concatenate([xs_all[p].reshape(rows, CW), xs_all[p + 1].reshape(rows, CW)], axis=1)

    def add_score(p):
        score[...] += dot(refs[:, pixels(p, 2)], slab(p), 1, 1)

    def y_copy(src, p, way, k2, j):
        return remote(src, xs_all.at[p], y_ss.at[way, k2, j], y_rs.at[way, k2, j], up if way == 0 else dn)

    def y_wait(yy, way, k2, j):
        p = piece(yy, k2, j)
        remote(xs_all.at[p], xs_all.at[p], y_ss.at[way, k2, j], y_rs.at[way, k2, j], up).wait_recv()

    def f_copy(p, way, j):
        return remote(xs_all.at[p], xs_all.at[p], f_ss.at[way, j], f_rs.at[way, j], up if way == 0 else dn)

    def chunk_wait(j):
        ref = recv.at[j, :, pl.ds(0, nq - 1)]
        remote(ref, ref, a_ss.at[j], a_rs.at[j], sibling).wait_recv()
        pltpu.make_async_copy(sendbuf.at[j, :, q], recv.at[j, :, q], a_loc.at[j]).wait()

    def home(k2, j):
        return piece(y, k2, j) if j < nch else piece(y_far, k2, j - far_n)

    def own_copy(j):
        return pltpu.make_async_copy(recv.at[j, k], xs_all.at[home(k, j)], k_loc.at[j])

    def sib_copy(j):
        return remote(recv.at[j, other], xs_all.at[home(k, j)], k_ss.at[j], k_rs.at[j], sibling)

    def stage0(j):
        chunk_wait(j)
        sib_copy(j).start()
        own_copy(j).start()
        if j < nch:
            for way in range(2):
                y_copy(recv.at[j, k], piece(y, k, j), way, k, j).start()
        sib_copy(j).wait_recv()
        if j < nch:
            for way in range(2):
                y_copy(xs_all.at[piece(y, other, j)], piece(y, other, j), way, other, j).start()
        own_copy(j).wait()

    def stage1(j):
        y_wait(y_dn, 0, 0, j)
        if j < nch - far_n:
            f_copy(piece(y_dn, 0, j), 0, j).start()
        y_wait(y_up, 1, 1, j)
        if j < nch - far_n:
            f_copy(piece(y_up, 1, j), 1, j).start()
        if j % 2:
            for k2 in range(2):
                add_score(piece(y, k2, j - 1))
            add_score(piece(y_dn, 0, j - 1))
            add_score(piece(y_up, 1, j - 1))
        y_wait(y_dn, 0, 1, j)
        y_wait(y_up, 1, 0, j)
        if j % 2:
            add_score(piece(y_dn, 1, j - 1))
            add_score(piece(y_up, 0, j - 1))

    def stage2(j):
        if j < nch - far_n:
            for way in range(2):
                f_copy(piece(y_far, way, j), way, j).wait_recv()
        if j % 2:
            for way in range(2):
                add_score(piece(y_far, way, j - 1))

    for j in range(nch):
        stage0(j)
        if j >= 1:
            stage1(j - 1)
        if 2 <= j and j - 2 < nch - far_n - far_n % 2:
            stage2(j - 2)
    stage1(nch - 1)
    for j in range(nch, n_chunk):
        stage0(j)
    for j in range(nch - 2 if nch - 2 < nch - far_n - far_n % 2 else nch - far_n - far_n % 2, nch):
        stage2(j)

    facts_done.wait_recv()
    known = by_chip(own_lanes(ptab[...]))
    half = 0.5 * jnp.sum(hnorm[...], axis=1, keepdims=True)
    s = known[0:1] * (score[...] - half)
    score[...] = s
    top = jnp.max(s, axis=0, keepdims=True)
    total = jnp.sum(jnp.exp(s - top), axis=0, keepdims=True)
    stat[y] = jnp.concatenate([top, total], axis=0)

    def share(i, c):
        remote(stat.at[y], stat.at[y], s_ss, s_rs, ((y + i) % ny, d)).start()
        return c

    lax.fori_loop(1, ny, share, 0)
    mate = known[1:2] * 8.0 + known[2:3]
    mate = jnp.concatenate([mate[:, w * 128:(w + 1) * 128] for w in range(nw)], axis=0)
    all_stat = stat.at[pl.ds(0, ny - 1)]
    remote(all_stat, all_stat, s_ss, s_rs, sibling).wait_recv()
    tops = [stat[yy, 0:1] for yy in range(ny)]
    high = functools.reduce(jnp.maximum, tops)
    mine = high + jnp.log(sum(stat[yy, 1:2] * jnp.exp(tops[yy] - high) for yy in range(ny)))
    mine = jnp.concatenate([mine[:, w * 128:(w + 1) * 128] for w in range(nw)], axis=0)

    lrow[...] = mine

    def spread_sums(i, c):
        remote(lrow, ltab.at[d], b_ss, b_rs, (y, (d + i) % n_bin)).start()
        return c

    lax.fori_loop(1, n_bin, spread_sums, 0)
    ltab[d] = mine
    all_sums = ltab.at[pl.ds(0, n_bin - 1)]
    remote(all_sums, all_sums, b_ss, b_rs, sibling).wait_recv()
    sums = ltab[...]
    slot = iota((nw, 128), 1) & 7
    key = iota(sums.shape, 0) * 8 + (iota(sums.shape, 2) & 7)
    key = key.astype(F32)
    theirs = jnp.zeros((nw, 128), F32)
    for delta in range(1 - SLOTS, SLOTS):
        asked = pltpu.roll(mate, delta % 128, 1)
        asked = jnp.where((slot - delta >= 0) & (slot - delta < SLOTS), asked, -1.0)
        found = jnp.sum(jnp.where(key == asked[None], sums, 0.0), axis=0)
        theirs = theirs + pltpu.roll(found, (-delta) % 128, 1)
    high = jnp.maximum(mine, theirs)
    log = high + jnp.log(jnp.exp(mine - high) + jnp.exp(theirs - high))
    log = jnp.concatenate([log[w:w + 1] for w in range(nw)], axis=1)
    weight[...] = (n_ref * jnp.exp(score[...] - log)).astype(BF16)

    windows(dsend, stat[y][1:2] * jnp.exp(stat[y][0:1] - log))

    def send_prob(i, c):
        d2 = (d + i) % n_bin
        remote(dsend.at[d2 // 16], dtab.at[d], d_ss, d_rs, (y, d2)).start()
        return c

    lax.fori_loop(1, n_bin, send_prob, 0)
    dtab[d] = dsend[d // 16]
    prob_done = remote(dtab.at[pl.ds(0, n_bin - 1)], dtab.at[pl.ds(0, n_bin - 1)], d_ss, d_rs, sibling)

    ld_int.wait()

    def sib_send(t):
        return remote(vb.at[t, :, other], sib.at[t], v_ss.at[t], v_rs.at[t], sibling)

    def x_send(t, i):
        x2 = (x + nx - 1 - i) % nx
        return remote(xs.at[t, i], xr.at[t, i], x_ss.at[t], x_rs.at[t], (y, (x2 * nz + z) * 2 + k))

    def x_all(t):
        ref = xr.at[t]
        return remote(ref, ref, x_ss.at[t], x_rs.at[t], sibling)

    def z_send(t):
        z2 = (z + nz - 1 - t) % nz
        return remote(zs.at[t], zr.at[t], z_ss.at[t], z_rs.at[t], (y, (x * nz + z2) * 2 + k))

    def insert(t):
        chips = [((x + nx - 1 - i) % nx) * nz + (z + nz - 1 - t) % nz for i in range(nx)]
        images = [dot(weight[...], slab(2 * c)).astype(BF16) for c in chips]
        sums = [dot(onehot[2 * c + h], im[:, h * LINE:(h + 1) * LINE]) for c, im in zip(chips, images) for h in (0, 1)]
        out = []
        for i in range(nx):
            for h in range(2):
                band = sums[2 * i + h]
                hi = band.astype(BF16)
                low = (band - hi.astype(F32)).astype(BF16)
                block = interp[2 * chips[i] + h]
                out.append(dot(jnp.concatenate([hi, low], axis=1), jnp.concatenate([block, block], axis=0)))
        for i in range(nx):
            for h in range(2):
                vb[t, i, h] = out[2 * i + h]

    def step(t, c):
        @pl.when(t < nz)
        def _():
            insert(t)
            sib_send(t).start()

        @pl.when((t >= 1) & (t <= nz))
        def _():
            u = t - 1
            sib_send(u).wait_recv()

            def one(i, c):
                xs[u, i] = (vb[u, i, k] + sib[u, i]).astype(BF16)
                x_send(u, i).start()
                return c

            lax.fori_loop(0, nx - 1, one, 0)

        @pl.when(t >= 2)
        def _():
            u = t - 2
            x_all(u).wait_recv()
            total = vb[u, nx - 1, k] + sib[u, nx - 1]
            for i in range(nx - 1):
                total += xr[u, i].astype(F32)

            @pl.when(u < nz - 1)
            def _():
                zs[u] = total.astype(BF16)
                z_send(u).start()

            @pl.when(u == nz - 1)
            def _():
                vol_ref[...] = total

        return c

    lax.fori_loop(0, nz + 2, step, 0)

    prob_done.wait_recv()
    t = own_lanes(dtab[...]).reshape(nq, 2, 128)
    t = by_chip(t)
    found = jnp.zeros((8, 2 * pairs), F32)
    for kb in range(2):
        cut = jnp.concatenate(thirds(t[kb:kb + 1]) + (jnp.zeros((5, rows), BF16),), axis=0)
        found += dot(cut, g2[kb])
    found = (found[2:3] + found[1:2]) + found[0:1]
    found = jnp.where(k == 0, found[:, :pairs], found[:, pairs:])
    prob_ref[...] = found[:, :part] + found[:, part:]

    def z_add(t, c):
        z_send(t).wait_recv()
        vol_ref[...] += zr[t].astype(F32)
        return c

    lax.fori_loop(0, nz - 1, z_add, 0)

    for e in ex:
        e.wait_send()
    facts_done.wait_send()
    remote(all_stat, all_stat, s_ss, s_rs, sibling).wait_send()
    remote(all_sums, all_sums, b_ss, b_rs, sibling).wait_send()
    prob_done.wait_send()
    for j in range(n_chunk):
        ref = recv.at[j, :, pl.ds(0, nq - 1)]
        remote(ref, ref, a_ss.at[j], a_rs.at[j], sibling).wait_send()
        sib_copy(j).wait_send()
    for j in range(nch):
        for way in range(2):
            y_copy(recv.at[j, k], piece(y, k, j), way, k, j).wait_send()
            y_copy(xs_all.at[piece(y, other, j)], piece(y, other, j), way, other, j).wait_send()
    for j in range(nch - far_n):
        f_copy(piece(y_dn, 0, j), 0, j).wait_send()
        f_copy(piece(y_up, 1, j), 1, j).wait_send()

    def v_done(t, c):
        sib_send(t).wait_send()
        x_all(t).wait_send()
        return c

    lax.fori_loop(0, nz, v_done, 0)
    lax.fori_loop(0, nz - 1, lambda t, c: (z_send(t).wait_send(), c)[1], 0)


def local(nz, images, bin_lists, precision, references, line_index, interp_blocks):
    ny, n_ptcl = lax.axis_size("cls"), lax.axis_size("ptcl")
    nq = n_ptcl // 2
    nx = nq // nz
    part, pixels = images.shape
    n_ref = references.shape[1]
    n_line = interp_blocks.shape[0]
    nch = pixels // (2 * ny * CW)
    n_chunk = nch + FAR
    rows = nq * 16
    nw = rows // 128
    vmem, dma = pltpu.VMEM, pltpu.SemaphoreType.DMA
    whole = pl.BlockSpec(memory_space=pltpu.VMEM)
    far = pl.BlockSpec(memory_space=pl.ANY)
    flops = 4 * n_ref * rows * pixels
    prob, volume = pl.pallas_call(
        functools.partial(kernel, ny, nx, nz, nch, FAR),
        out_shape=(jax.ShapeDtypeStruct((1, part), F32), jax.ShapeDtypeStruct((LINE, LINE), F32)),
        in_specs=[far, whole, whole, far, whole, far],
        out_specs=(whole, whole),
        scratch_shapes=[
            vmem((2, part, n_chunk * CW), BF16),
            vmem((2, 8, part), F32),
            vmem((2 * rows, 2 * part), BF16),
            vmem((2, rows, 4 * part), BF16),
            vmem((n_chunk, 2, nq, 16, CW), BF16),
            vmem((n_chunk, 2, nq, 16, CW), BF16),
            vmem((2 * ny * nch, nq, 16, CW), BF16),
            vmem((n_ref, pixels), BF16),
            vmem((n_line, LINE, n_ref), BF16),
            vmem((n_line, LINE, LINE), BF16),
            vmem((n_ref, rows), F32),
            vmem((n_ref, rows), BF16),
            vmem((n_ref, 128), F32),
            vmem((nw, 8, 128), F32), vmem((nq, 8, 128), F32),
            vmem((ny, 2, rows), F32),
            vmem((nw, 128), F32), vmem((n_ptcl, nw, 128), F32),
            vmem((nw, 1, 128), F32), vmem((n_ptcl, 1, 128), F32),
            vmem((nz, nx, 2, LINE, LINE), F32),
            vmem((nz, nx, LINE, LINE), F32),
            vmem((nz, nx - 1, LINE, LINE), BF16), vmem((nz, nx - 1, LINE, LINE), BF16),
            vmem((nz - 1, LINE, LINE), BF16), vmem((nz - 1, LINE, LINE), BF16),
            dma((4,)), dma((3,)), dma((3,)),
            dma((n_chunk,)), dma((n_chunk,)), dma((n_chunk,)),
            dma(()), dma(()),
            dma((n_chunk,)), dma((n_chunk,)), dma((n_chunk,)),
            dma((2, 2, nch)), dma((2, 2, nch)),
            dma((2, nch)), dma((2, nch)),
            dma(()), dma(()), dma(()), dma(()), dma(()), dma(()),
            dma((nz,)), dma((nz,)), dma((nz,)), dma((nz,)), dma((nz - 1,)), dma((nz - 1,)),
        ],
        compiler_params=pltpu.CompilerParams(collective_id=0, has_side_effects=True, vmem_limit_bytes=58 << 20),
        cost_estimate=pl.CostEstimate(flops=flops, bytes_accessed=n_ref * pixels * 2, transcendentals=0),
    )(images, bin_lists.T, precision.reshape(1, part), references[0], line_index[0].T, interp_blocks)
    return prob.reshape(part, 1), volume[None]


def solution(mesh, nz=NZ):
    in_specs = (
        P("ptcl", None),
        P("ptcl", None),
        P("ptcl"),
        P("cls", "ptcl", None),
        P("cls", "ptcl", None),
        P(),
    )
    out_specs = (P("ptcl", "cls"), P("cls", "ptcl", None))
    return jax.shard_map(functools.partial(local, nz), mesh=mesh, in_specs=in_specs, out_specs=out_specs,
                         check_vma=False)
```

time: 162 us -> 139 us (0.86)
  Pallas kernels: 156 us -> 135 us
  other arithmetic: 2 us -> 0 us
    pallas_call x1, Pallas kernels: 156 us -> 135 us  [local(): pl.pallas_call(functools.partial(kernel, ny, nx, nz, nch, FAR), out_shape...]
where the time goes in v2:
time: 139 us; the launch traced here: 138 us
  Pallas kernels  135 us (97%)
  local copies, waits for them, and re-layouts  2.59 us (2%)
    pallas_call x1, Pallas kernels, local(): pl.pallas_call(functools.partial(kernel, ny, nx, nz, nch, FAR), out_shape...  135 us

profile of v2, /device:TPU:8, one launch (start us, length us, event | category | flops | bytes accessed | tf_op | source)
XLA Modules:
  0.0 138.3 jit_solution(7065525514236863382)
XLA Ops:
  0.6 135.0 %shard_map.77 = (f32[1,128]{1,0:T(1,128)}, f32[128,128]{1,0:T(8,128)}) custom-call(bf16[128,8192]{1,0:T(8,128)(2,1)} %img_hbm.1, s32[2,128]{1,0:T(2,128)} %bitcast.11, bf16[1,128]{1,0:T(2,128)(2,1)} %bitcast.12, bf16[512,8192]{1,0:T(8,128)(2,1)} %bitcast.9, s32[64,512]{1,0:T(8,128)} %bitcast.10, bf16[64,128,128]{2,1,0:T(8,128)(2,1)} %interp_hbm.1), custom_call_target="tpu_custom_call" | custom-call | flops 8589934592 | bytes 8388608 | tf_op jit(solution)/shard_map/pallas_call | solution.py:467
  135.7 1.1 copy.10
  136.8 1.5 %copy.11 = f32[1,128,128]{2,1,0:T(8,128)} copy(f32[1,128,128]{2,1,0:T(8,128)} %bitcast.8) | data formatting | bytes 131072

commit v3 on v2

v3 whole, which is shorter than its diff:
```python
import functools

import jax
import jax.numpy as jnp
from jax import lax
from jax.experimental import pallas as pl
from jax.experimental.pallas import tpu as pltpu
from jax.sharding import PartitionSpec as P

MESH = pl.DeviceIdType.MESH
F32, BF16, I32 = jnp.float32, jnp.bfloat16, jnp.int32
NZ = 8
CW = 128
FAR = 4
LAG = 4
LINE = 128
SLOTS = 8


def iota(shape, dim):
    return lax.broadcasted_iota(I32, shape, dim)


def dot(a, b, ca=1, cb=0):
    return lax.dot_general(a, b, (((ca,), (cb,)), ((), ())), preferred_element_type=F32)


def thirds(v):
    hi = v.astype(BF16)
    rest = v - hi.astype(F32)
    mid = rest.astype(BF16)
    low = (rest - mid.astype(F32)).astype(BF16)
    return hi, mid, low


def kernel(ny, nx, nz, nd, far_n, img_hbm, bins_ref, prec_ref, refs_hbm, idx_hbm, interp_hbm, prob_ref, vol_ref,
           img, g, g2, sendbuf, recv, xs_all, refs, idx, onehot, interp, score, weight, hnorm,
           psend, ptab, stat, lrow, ltab, dsend, dtab, vb, sib, xs, xr, zs, zr,
           load_sem, a_ss, a_rs, a_loc, p_ss, p_rs,
           y_ss, y_rs, f_ss, f_rs, s_ss, s_rs, b_ss, b_rs, d_ss, d_rs,
           v_ss, v_rs, x_ss, x_rs, z_ss, z_rs):
    nq = nx * nz
    y, d = lax.axis_index("cls"), lax.axis_index("ptcl")
    q, k = d // 2, d % 2
    x, z = q // nz, q % nz
    other = 1 - k
    part = bins_ref.shape[1]
    n_bin, pairs = nq * 2, 2 * part
    n_pair = nd + far_n
    n_ref = refs.shape[0]
    rows = n_bin * SLOTS
    nw = rows // 128
    per_w = 128 // SLOTS
    sibling = (y, q * 2 + other)
    y_up, y_dn, y_far = (y + 1) % ny, (y + ny - 1) % ny, (y + 2) % ny
    up, dn = (y_up, d), (y_dn, d)

    def remote(src, dst, ss, rs, dev):
        return pltpu.make_async_remote_copy(src_ref=src, dst_ref=dst, send_sem=ss, recv_sem=rs,
                                            device_id=dev, device_id_type=MESH)

    def piece(yy, h, m):
        return (yy * nd + m) * 2 + h

    def pixels(p, count):
        return pl.ds(pl.multiple_of(p * CW, 2 * CW), count * CW)

    bar = pltpu.get_barrier_semaphore()

    def greet(i, c):
        pl.semaphore_signal(bar, inc=1, device_id=(y, (d + i) % n_bin), device_id_type=MESH)
        return c

    def greet_y(i, c):
        pl.semaphore_signal(bar, inc=1, device_id=((y + i) % ny, d), device_id_type=MESH)
        return c

    lax.fori_loop(1, n_bin, greet, 0)
    lax.fori_loop(1, ny, greet_y, 0)

    loads = [
        pltpu.make_async_copy(img_hbm.at[:, pixels(piece(y, 0, 0), 2 * nd)], img.at[:, pl.ds(0, 2 * nd * CW)],
                              load_sem.at[0]),
        pltpu.make_async_copy(img_hbm.at[:, pixels(piece(y_far, 0, nd - far_n), 2 * far_n)],
                              img.at[:, pl.ds(2 * nd * CW, 2 * far_n * CW)], load_sem.at[1]),
        pltpu.make_async_copy(idx_hbm, idx, load_sem.at[2]),
        pltpu.make_async_copy(refs_hbm, refs, load_sem.at[3]),
        pltpu.make_async_copy(interp_hbm, interp, load_sem.at[4]),
    ]
    for ld in loads:
        ld.start()

    own_bins = bins_ref[...].astype(F32)
    bins = jnp.concatenate([own_bins[0:1], own_bins[1:2]], axis=1)
    before = (iota((pairs, pairs), 0) < iota((pairs, pairs), 1)).astype(F32).astype(BF16)
    named = (iota((n_bin, pairs), 0).astype(F32) == bins).astype(F32)
    rank = named * dot(named.astype(BF16), before)
    expand = (lax.shift_right_logical(iota((rows, n_bin), 0), 3) == iota((rows, n_bin), 1)).astype(F32).astype(BF16)
    spread = dot(expand, (named + rank).astype(BF16))
    hit = (spread == ((iota((rows, pairs), 0) & 7) + 1).astype(F32)).astype(F32)
    g2[...] = hit.astype(BF16)
    g[...] = (hit[:, :part] + hit[:, part:]).astype(BF16)

    def gather(m):
        out = dot(g[...], img[:, 2 * m * CW:2 * (m + 1) * CW])
        halves = [out[:, h * CW:(h + 1) * CW].reshape(n_bin, SLOTS, CW) for h in range(2)]
        sendbuf[:, m] = jnp.concatenate(halves, axis=1).astype(BF16)

    def own_part(m, n, c):
        return pltpu.make_async_copy(sendbuf.at[d, pl.ds(m, n)], recv.at[d, pl.ds(m, n)], a_loc.at[c])

    def send_chunk(m, n, c):
        def send(i, carry):
            d2 = (d + i) % n_bin
            remote(sendbuf.at[d2, pl.ds(m, n)], recv.at[d, pl.ds(m, n)], a_ss.at[c], a_rs.at[c], (y, d2)).start()
            return carry

        lax.fori_loop(1, n_bin, send, 0)
        own_part(m, n, c).start()

    def chunk_all(m, n, c):
        ref = recv.at[pl.ds(0, n_bin - 1), pl.ds(m, n)]
        return remote(ref, ref, a_ss.at[c], a_rs.at[c], sibling)

    chunks = [(m, 1) for m in range(n_pair)]
    loads[0].wait()
    gather(0)
    pl.semaphore_wait(bar, n_bin - 1 + ny - 1)
    for c, (m, n) in enumerate(chunks):
        if c == nd:
            loads[1].wait()
        if c:
            gather(m)
        send_chunk(m, n, c)

    def own_lanes(t):
        axis = t.ndim - 1
        t = jnp.where(lax.shift_right_logical(iota(t.shape, axis), 3) == d % per_w, t, 0.0)
        for s in (64, 32, 16, 8):
            t = t + pltpu.roll(t, s, axis)
        return t

    def by_device(t):
        t = t.reshape(nw, per_w, t.shape[1], 128)
        return jnp.sum(jnp.where(lax.shift_right_logical(iota(t.shape, 3), 3) == iota(t.shape, 1), t, 0.0), axis=1)

    def in_row(t):
        return jnp.concatenate([t[w:w + 1] for w in range(nw)], axis=1)

    def in_windows(t):
        return jnp.concatenate([t[:, w * 128:(w + 1) * 128] for w in range(nw)], axis=0)

    prec = prec_ref[...].astype(F32)
    ranks = jnp.sum(rank, axis=0, keepdims=True)
    facts = [[prec, prec], [own_bins[1:2], own_bins[0:1]], [ranks[:, part:], ranks[:, :part]]]
    facts = [jnp.concatenate(v, axis=1) for v in facts]
    facts = jnp.concatenate(facts + [jnp.zeros((5, pairs), F32)], axis=0).astype(BF16)
    facts = dot(facts, g2[...], 1, 1)
    facts = jnp.concatenate([facts[0:1], facts[1:2] * SLOTS + facts[2:3]], axis=0)
    for w in range(nw):
        psend[w] = facts[:, w * 128:(w + 1) * 128]

    def send_facts(i, c):
        d2 = (d + i) % n_bin
        remote(psend.at[d2 // per_w], ptab.at[d], p_ss, p_rs, (y, d2)).start()
        return c

    lax.fori_loop(1, n_bin, send_facts, 0)
    ptab[d] = psend[d // per_w]
    facts_done = remote(ptab.at[pl.ds(0, n_bin - 1)], ptab.at[pl.ds(0, n_bin - 1)], p_ss, p_rs, sibling)

    hnorm[...] = jnp.zeros_like(hnorm)
    score[...] = jnp.zeros_like(score)

    def aside(m):
        def norm(i, c):
            v = refs[:, pl.ds(pl.multiple_of(i * 128, 128), 128)].astype(F32)
            hnorm[...] += v * v
            return c

        def bands(i, c):
            onehot[i] = (iota((LINE, n_ref), 0) == idx[pl.ds(i, 1), :]).astype(F32).astype(BF16)
            return c

        count = onehot.shape[0] // nd
        lax.fori_loop(m * count, (m + 1) * count, norm, 0)
        lax.fori_loop(m * count, (m + 1) * count, bands, 0)

    def slab(p):
        return jnp.concatenate([xs_all[p].reshape(rows, CW), xs_all[p + 1].reshape(rows, CW)], axis=1)

    def add_score(p):
        score[...] += dot(refs[:, pixels(p, 2)], slab(p), 1, 1)

    def y_copy(way, h, m):
        ref = xs_all.at[piece(y, h, m)]
        return remote(ref, ref, y_ss.at[way, h, m], y_rs.at[way, h, m], up if way == 0 else dn)

    def f_copy(way, m):
        ref = xs_all.at[piece(y_dn if way == 0 else y_up, way, m)]
        return remote(ref, ref, f_ss.at[way, m], f_rs.at[way, m], up if way == 0 else dn)

    def stage0(c):
        m, n = chunks[c]
        chunk_all(m, n, c).wait_recv()
        own_part(m, n, c).wait()
        for i in range(m, m + n):
            t = recv[:, i].astype(F32)
            for h in range(2):
                p = piece(y, h, i) if i < nd else piece(y_far, h, i - far_n)
                xs_all[p] = t[:, h * SLOTS:(h + 1) * SLOTS].reshape(nq, 16, CW).astype(BF16)
            if i < nd:
                for h in range(2):
                    for way in range(2):
                        y_copy(way, h, i).start()

    def stage1(m):
        for way in range(2):
            y_copy(way, way, m).wait_recv()
            if m < nd - far_n:
                f_copy(way, m).start()
        add_score(piece(y, 0, m))
        for way in range(2):
            y_copy(way, 1 - way, m).wait_recv()
        add_score(piece(y_dn, 0, m))
        add_score(piece(y_up, 0, m))

    def stage2(m):
        if m < nd - far_n:
            for way in range(2):
                f_copy(way, m).wait_recv()
        add_score(piece(y_far, 0, m))

    loads[2].wait()
    loads[3].wait()
    for m in range(nd):
        stage0(m)
        if m >= 1:
            stage1(m - 1)
        if 2 <= m < nd - far_n + 2:
            stage2(m - 2)
        aside(m)
    stage1(nd - 1)
    for c in range(nd, n_pair):
        stage0(c)
    for m in range(min(nd - 2, nd - far_n), nd):
        stage2(m)

    facts_done.wait_recv()
    known = by_device(own_lanes(ptab[...]))
    scale = in_row(known[:, 0])
    mate = known[:, 1]
    half = 0.5 * jnp.sum(hnorm[...], axis=1, keepdims=True)
    s = scale * (score[...] - half)
    score[...] = s
    top = jnp.max(s, axis=0, keepdims=True)
    total = jnp.sum(jnp.exp(s - top), axis=0, keepdims=True)
    stat[y] = jnp.concatenate([top, total], axis=0)

    def share(i, c):
        remote(stat.at[y], stat.at[y], s_ss, s_rs, ((y + i) % ny, d)).start()
        return c

    lax.fori_loop(1, ny, share, 0)
    all_stat = stat.at[pl.ds(0, ny - 1)]
    remote(all_stat, all_stat, s_ss, s_rs, sibling).wait_recv()
    tops = [stat[yy, 0:1] for yy in range(ny)]
    high = functools.reduce(jnp.maximum, tops)
    mine = in_windows(high + jnp.log(sum(stat[yy, 1:2] * jnp.exp(tops[yy] - high) for yy in range(ny))))

    lrow[...] = mine

    def spread_sums(i, c):
        remote(lrow, ltab.at[d], b_ss, b_rs, (y, (d + i) % n_bin)).start()
        return c

    lax.fori_loop(1, n_bin, spread_sums, 0)
    ltab[d] = mine
    all_sums = ltab.at[pl.ds(0, n_bin - 1)]
    remote(all_sums, all_sums, b_ss, b_rs, sibling).wait_recv()
    sums = ltab[...]
    slot = iota((nw, 128), 1) & 7
    key = (iota(sums.shape, 0) * SLOTS + (iota(sums.shape, 2) & 7)).astype(F32)
    theirs = jnp.zeros((nw, 128), F32)
    for delta in range(1 - SLOTS, SLOTS):
        asked = pltpu.roll(mate, delta % 128, 1)
        asked = jnp.where((slot - delta >= 0) & (slot - delta < SLOTS), asked, -1.0)
        found = jnp.sum(jnp.where(key == asked[None], sums, 0.0), axis=0)
        theirs = theirs + pltpu.roll(found, (-delta) % 128, 1)
    high = jnp.maximum(mine, theirs)
    log = in_row(high + jnp.log(jnp.exp(mine - high) + jnp.exp(theirs - high)))
    weight[...] = (n_ref * jnp.exp(score[...] - log)).astype(BF16)

    loads[4].wait()

    def sib_send(t):
        return remote(vb.at[t, :, other], sib.at[t], v_ss.at[t], v_rs.at[t], sibling)

    def x_send(t, i):
        x2 = (x + nx - 1 - i) % nx
        return remote(xs.at[t, i], xr.at[t, i], x_ss.at[t], x_rs.at[t], (y, (x2 * nz + z) * 2 + k))

    def x_all(t):
        ref = xr.at[t]
        return remote(ref, ref, x_ss.at[t], x_rs.at[t], sibling)

    def z_send(t):
        z2 = (z + nz - 1 - t) % nz
        return remote(zs.at[t], zr.at[t], z_ss.at[t], z_rs.at[t], (y, (x * nz + z2) * 2 + k))

    def insert(t):
        chips = [((x + nx - 1 - i) % nx) * nz + (z + nz - 1 - t) % nz for i in range(nx)]
        images = [dot(weight[...], slab(2 * c)).astype(BF16) for c in chips]
        sums = [dot(onehot[2 * c + h], im[:, h * LINE:(h + 1) * LINE]) for c, im in zip(chips, images) for h in (0, 1)]
        out = []
        for i in range(nx):
            for h in range(2):
                band = sums[2 * i + h]
                hi = band.astype(BF16)
                low = (band - hi.astype(F32)).astype(BF16)
                block = interp[2 * chips[i] + h]
                out.append(dot(jnp.concatenate([hi, low], axis=1), jnp.concatenate([block, block], axis=0)))
        for i in range(nx):
            for h in range(2):
                vb[t, i, h] = out[2 * i + h]

    def step(t, c):
        @pl.when(t < nz)
        def _():
            insert(t)
            sib_send(t).start()

        @pl.when((t >= 1) & (t <= nz))
        def _():
            u = t - 1
            sib_send(u).wait_recv()

            def one(i, c):
                xs[u, i] = (vb[u, i, k] + sib[u, i]).astype(BF16)
                x_send(u, i).start()
                return c

            lax.fori_loop(0, nx - 1, one, 0)

        @pl.when(t >= LAG)
        def _():
            u = t - LAG
            x_all(u).wait_recv()
            total = vb[u, nx - 1, k] + sib[u, nx - 1]
            for i in range(nx - 1):
                total += xr[u, i].astype(F32)

            @pl.when(u < nz - 1)
            def _():
                zs[u] = total.astype(BF16)
                z_send(u).start()

            @pl.when(u == nz - 1)
            def _():
                vol_ref[...] = total

        return c

    lax.fori_loop(0, 2, step, 0)

    chance = stat[y][1:2] * jnp.exp(stat[y][0:1] - log)
    for w in range(nw):
        dsend[w] = chance[:, w * 128:(w + 1) * 128]

    def send_prob(i, c):
        d2 = (d + i) % n_bin
        remote(dsend.at[d2 // per_w], dtab.at[d], d_ss, d_rs, (y, d2)).start()
        return c

    lax.fori_loop(1, n_bin, send_prob, 0)
    dtab[d] = dsend[d // per_w]
    prob_done = remote(dtab.at[pl.ds(0, n_bin - 1)], dtab.at[pl.ds(0, n_bin - 1)], d_ss, d_rs, sibling)

    lax.fori_loop(2, nz + 1, step, 0)

    prob_done.wait_recv()
    found = in_row(by_device(own_lanes(dtab[...]))[:, 0])
    found = dot(jnp.concatenate(thirds(found) + (jnp.zeros((5, rows), BF16),), axis=0), g2[...])
    found = (found[2:3] + found[1:2]) + found[0:1]
    prob_ref[...] = found[:, :part] + found[:, part:]

    lax.fori_loop(nz + 1, nz + LAG, step, 0)

    def z_add(t, c):
        z_send(t).wait_recv()
        vol_ref[...] += zr[t].astype(F32)
        return c

    lax.fori_loop(0, nz - 1, z_add, 0)

    facts_done.wait_send()
    remote(all_stat, all_stat, s_ss, s_rs, sibling).wait_send()
    remote(all_sums, all_sums, b_ss, b_rs, sibling).wait_send()
    prob_done.wait_send()
    for c, (m, n) in enumerate(chunks):
        chunk_all(m, n, c).wait_send()
    for m in range(nd):
        for way in range(2):
            for h in range(2):
                y_copy(way, h, m).wait_send()
            if m < nd - far_n:
                f_copy(way, m).wait_send()

    def v_done(t, c):
        sib_send(t).wait_send()
        x_all(t).wait_send()
        return c

    lax.fori_loop(0, nz, v_done, 0)
    lax.fori_loop(0, nz - 1, lambda t, c: (z_send(t).wait_send(), c)[1], 0)


def local(nz, images, bin_lists, precision, references, line_index, interp_blocks):
    ny, n_ptcl = lax.axis_size("cls"), lax.axis_size("ptcl")
    nq = n_ptcl // 2
    nx = nq // nz
    part, pixels = images.shape
    n_ref = references.shape[1]
    n_line = interp_blocks.shape[0]
    nd = pixels // (2 * ny * CW)
    n_pair = nd + FAR
    rows = n_ptcl * SLOTS
    nw = rows // 128
    vmem, dma = pltpu.VMEM, pltpu.SemaphoreType.DMA
    whole = pl.BlockSpec(memory_space=pltpu.VMEM)
    far = pl.BlockSpec(memory_space=pl.ANY)
    flops = 4 * n_ref * rows * pixels
    prob, volume = pl.pallas_call(
        functools.partial(kernel, ny, nx, nz, nd, FAR),
        out_shape=(jax.ShapeDtypeStruct((1, part), F32), jax.ShapeDtypeStruct((LINE, LINE), F32)),
        in_specs=[far, whole, whole, far, far, far],
        out_specs=(whole, whole),
        scratch_shapes=[
            vmem((part, 2 * n_pair * CW), BF16),
            vmem((rows, part), BF16),
            vmem((rows, 2 * part), BF16),
            vmem((n_ptcl, n_pair, 16, CW), BF16),
            vmem((n_ptcl, n_pair, 16, CW), BF16),
            vmem((2 * ny * nd, nq, 16, CW), BF16),
            vmem((n_ref, pixels), BF16),
            vmem((n_line, n_ref), I32),
            vmem((n_line, LINE, n_ref), BF16),
            vmem((n_line, LINE, LINE), BF16),
            vmem((n_ref, rows), F32),
            vmem((n_ref, rows), BF16),
            vmem((n_ref, 128), F32),
            vmem((nw, 2, 128), F32), vmem((n_ptcl, 2, 128), F32),
            vmem((ny, 2, rows), F32),
            vmem((nw, 128), F32), vmem((n_ptcl, nw, 128), F32),
            vmem((nw, 1, 128), F32), vmem((n_ptcl, 1, 128), F32),
            vmem((nz, nx, 2, LINE, LINE), F32),
            vmem((nz, nx, LINE, LINE), F32),
            vmem((nz, nx - 1, LINE, LINE), BF16), vmem((nz, nx - 1, LINE, LINE), BF16),
            vmem((nz - 1, LINE, LINE), BF16), vmem((nz - 1, LINE, LINE), BF16),
            dma((5,)),
            dma((n_pair,)), dma((n_pair,)), dma((n_pair,)),
            dma(()), dma(()),
            dma((2, 2, nd)), dma((2, 2, nd)),
            dma((2, nd)), dma((2, nd)),
            dma(()), dma(()), dma(()), dma(()), dma(()), dma(()),
            dma((nz,)), dma((nz,)), dma((nz,)), dma((nz,)), dma((nz - 1,)), dma((nz - 1,)),
        ],
        compiler_params=pltpu.CompilerParams(collective_id=0, has_side_effects=True, vmem_limit_bytes=58 << 20),
        cost_estimate=pl.CostEstimate(flops=flops, bytes_accessed=n_ref * pixels * 2, transcendentals=0),
    )(images, bin_lists.T, precision.reshape(1, part), references[0], line_index[0].T, interp_blocks)
    return prob.reshape(part, 1), volume[None]


def solution(mesh, nz=NZ):
    in_specs = (
        P("ptcl", None),
        P("ptcl", None),
        P("ptcl"),
        P("cls", "ptcl", None),
        P("cls", "ptcl", None),
        P(),
    )
    out_specs = (P("ptcl", "cls"), P("cls", "ptcl", None))
    return jax.shard_map(functools.partial(local, nz), mesh=mesh, in_specs=in_specs, out_specs=out_specs,
                         check_vma=False)
```

time: 139 us -> 127 us (0.914); the launches traced: 138 us -> 124 us
  Pallas kernels: 135 us -> 121 us
    pallas_call x1, Pallas kernels: 135 us -> 121 us  [local(): pl.pallas_call(functools.partial(kernel, ny, nx, nz, nd, FAR), out_shape=...]
where the time goes in v3:
time: 127 us; the launch traced here: 124 us
  Pallas kernels  121 us (95%)
  local copies, waits for them, and re-layouts  2.59 us (2%)
    pallas_call x1, Pallas kernels, local(): pl.pallas_call(functools.partial(kernel, ny, nx, nz, nd, FAR), out_shape=...  121 us
    unnamed x2, local copies, waits for them, and re-layouts  2.59 us

profile of v3, /device:TPU:8, one launch (start us, length us, event | category | flops | bytes accessed | tf_op | source)
XLA Modules:
  0.0 124.4 jit_solution(10435991951120594486)
XLA Ops:
  0.6 121.2 %shard_map.77 = (f32[1,128]{1,0:T(1,128)}, f32[128,128]{1,0:T(8,128)}) custom-call(bf16[128,8192]{1,0:T(8,128)(2,1)} %img_hbm.1, s32[2,128]{1,0:T(2,128)} %bitcast.11, bf16[1,128]{1,0:T(2,128)(2,1)} %bitcast.12, bf16[512,8192]{1,0:T(8,128)(2,1)} %bitcast.9, s32[64,512]{1,0:T(8,128)} %bitcast.10, bf16[64,128,128]{2,1,0:T(8,128)(2,1)} %interp_hbm.1), custom_call_target="tpu_custom_call" | custom-call | flops 8589934592 | bytes 8388608 | tf_op jit(solution)/shard_map/pallas_call | solution.py:433
  121.8 1.1 copy.10
  122.9 1.5 %copy.11 = f32[1,128,128]{2,1,0:T(8,128)} copy(f32[1,128,128]{2,1,0:T(8,128)} %bitcast.8) | data formatting | bytes 131072

commit v4 on v3

--- a/solution.py
+++ b/solution.py
@@ -12,7 +12,9 @@
 NZ = 8
 CW = 128
 FAR = 4
-LAG = 4
+HOLD = 2
+LAG = 5
+AHEAD = 5
 LINE = 128
 SLOTS = 8
 
@@ -33,10 +35,10 @@
     return hi, mid, low
 
 
-def kernel(ny, nx, nz, nd, far_n, img_hbm, bins_ref, prec_ref, refs_hbm, idx_hbm, interp_hbm, prob_ref, vol_ref,
-           img, g, g2, sendbuf, recv, xs_all, refs, idx, onehot, interp, score, weight, hnorm,
+def kernel(ny, nx, nz, nd, far_n, img_hbm, bins_hbm, prec_hbm, refs_hbm, idx_hbm, interp_hbm, prob_ref, vol_ref,
+           img, bins_ref, prec_ref, g, g2, sendbuf, recv, xs_all, refs, idx, onehot, interp, score, weight, hnorm,
            psend, ptab, stat, lrow, ltab, dsend, dtab, vb, sib, xs, xr, zs, zr,
-           load_sem, a_ss, a_rs, a_loc, p_ss, p_rs,
+           load_sem, a_ss, a_rs, a_loc, h_ss, h_rs, p_ss, p_rs,
            y_ss, y_rs, f_ss, f_rs, s_ss, s_rs, b_ss, b_rs, d_ss, d_rs,
            v_ss, v_rs, x_ss, x_rs, z_ss, z_rs):
     nq = nx * nz
@@ -79,17 +81,23 @@
     lax.fori_loop(1, ny, greet_y, 0)
 
     loads = [
-        pltpu.make_async_copy(img_hbm.at[:, pixels(piece(y, 0, 0), 2 * nd)], img.at[:, pl.ds(0, 2 * nd * CW)],
-                              load_sem.at[0]),
+        pltpu.make_async_copy(img_hbm.at[:, pixels(piece(y, 0, 1), 2 * nd - 2)],
+                              img.at[:, pl.ds(2 * CW, (2 * nd - 2) * CW)], load_sem.at[0]),
         pltpu.make_async_copy(img_hbm.at[:, pixels(piece(y_far, 0, nd - far_n), 2 * far_n)],
                               img.at[:, pl.ds(2 * nd * CW, 2 * far_n * CW)], load_sem.at[1]),
         pltpu.make_async_copy(idx_hbm, idx, load_sem.at[2]),
         pltpu.make_async_copy(refs_hbm, refs, load_sem.at[3]),
         pltpu.make_async_copy(interp_hbm, interp, load_sem.at[4]),
     ]
-    for ld in loads:
+    first = [
+        pltpu.make_async_copy(bins_hbm, bins_ref, load_sem.at[5]),
+        pltpu.make_async_copy(img_hbm.at[:, pixels(piece(y, 0, 0), 2)], img.at[:, pl.ds(0, 2 * CW)], load_sem.at[6]),
+        pltpu.make_async_copy(prec_hbm, prec_ref, load_sem.at[7]),
+    ]
+    for ld in first + loads:
         ld.start()
 
+    first[0].wait()
     own_bins = bins_ref[...].astype(F32)
     bins = jnp.concatenate([own_bins[0:1], own_bins[1:2]], axis=1)
     before = (iota((pairs, pairs), 0) < iota((pairs, pairs), 1)).astype(F32).astype(BF16)
@@ -122,16 +130,40 @@
         ref = recv.at[pl.ds(0, n_bin - 1), pl.ds(m, n)]
         return remote(ref, ref, a_ss.at[c], a_rs.at[c], sibling)
 
+    group = 2 * nz
+    steps_x = sorted(range(nx), key=lambda dx: min(dx, nx - dx))
+
+    def send_head(dx):
+        def send(i, carry):
+            d2 = ((x + dx) % nx) * group + (d + i) % group
+            remote(sendbuf.at[d2, pl.ds(0, 1)], recv.at[d, pl.ds(0, 1)], h_ss.at[dx], h_rs.at[dx], (y, d2)).start()
+            return carry
+
+        lax.fori_loop(0 if dx else 1, group, send, 0)
+
+    def head_all(dx):
+        ref = recv.at[pl.ds(0, group if dx else group - 1), pl.ds(0, 1)]
+        return remote(ref, ref, h_ss.at[dx], h_rs.at[dx], sibling)
+
     chunks = [(m, 1) for m in range(n_pair)]
-    loads[0].wait()
+    first[1].wait()
     gather(0)
     pl.semaphore_wait(bar, n_bin - 1 + ny - 1)
-    for c, (m, n) in enumerate(chunks):
+
+    def issue(c):
+        m, n = chunks[c]
+        if c == 1:
+            loads[0].wait()
         if c == nd:
             loads[1].wait()
-        if c:
-            gather(m)
+        gather(m)
         send_chunk(m, n, c)
+
+    own_part(0, 1, 0).start()
+    for dx in steps_x:
+        send_head(dx)
+    for c in range(1, min(AHEAD, n_pair)):
+        issue(c)
 
     def own_lanes(t):
         axis = t.ndim - 1
@@ -150,6 +182,7 @@
     def in_windows(t):
         return jnp.concatenate([t[:, w * 128:(w + 1) * 128] for w in range(nw)], axis=0)
 
+    first[2].wait()
     prec = prec_ref[...].astype(F32)
     ranks = jnp.sum(rank, axis=0, keepdims=True)
     facts = [[prec, prec], [own_bins[1:2], own_bins[0:1]], [ranks[:, part:], ranks[:, :part]]]
@@ -213,6 +246,24 @@
                 for h in range(2):
                     for way in range(2):
                         y_copy(way, h, i).start()
+        if c + AHEAD - 1 < n_pair:
+            issue(c + AHEAD - 1)
+
+    def head_copy(way, h, x_src):
+        ref = xs_all.at[piece(y, h, 0), pl.ds(x_src * nz, nz)]
+        return remote(ref, ref, y_ss.at[way, h, 0], y_rs.at[way, h, 0], up if way == 0 else dn)
+
+    def stage_head():
+        own_part(0, 1, 0).wait()
+        for dx in steps_x:
+            head_all(dx).wait_recv()
+            x_src = (x + nx - dx) % nx
+            t = recv[pl.ds(x_src * group, group), 0].astype(F32)
+            for h in range(2):
+                xs_all[piece(y, h, 0), pl.ds(x_src * nz, nz)] = (
+                    t[:, h * SLOTS:(h + 1) * SLOTS].reshape(nz, 16, CW).astype(BF16))
+                for way in range(2):
+                    head_copy(way, h, x_src).start()
 
     def stage1(m):
         for way in range(2):
@@ -234,24 +285,28 @@
     loads[2].wait()
     loads[3].wait()
     for m in range(nd):
-        stage0(m)
+        if m:
+            stage0(m)
+        else:
+            stage_head()
         if m >= 1:
             stage1(m - 1)
         if 2 <= m < nd - far_n + 2:
             stage2(m - 2)
         aside(m)
-    stage1(nd - 1)
-    for c in range(nd, n_pair):
-        stage0(c)
-    for m in range(min(nd - 2, nd - far_n), nd):
-        stage2(m)
-
+    score[...] -= 0.5 * jnp.sum(hnorm[...], axis=1, keepdims=True)
     facts_done.wait_recv()
     known = by_device(own_lanes(ptab[...]))
     scale = in_row(known[:, 0])
     mate = known[:, 1]
-    half = 0.5 * jnp.sum(hnorm[...], axis=1, keepdims=True)
-    s = scale * (score[...] - half)
+    stage1(nd - 1)
+    for m in range(nd - 2, nd - far_n):
+        stage2(m)
+    for c in range(nd, n_pair):
+        stage0(c)
+        stage2(c - far_n)
+
+    s = scale * score[...]
     score[...] = s
     top = jnp.max(s, axis=0, keepdims=True)
     total = jnp.sum(jnp.exp(s - top), axis=0, keepdims=True)
@@ -330,9 +385,9 @@
             insert(t)
             sib_send(t).start()
 
-        @pl.when((t >= 1) & (t <= nz))
+        @pl.when((t >= HOLD) & (t < nz + HOLD))
         def _():
-            u = t - 1
+            u = t - HOLD
             sib_send(u).wait_recv()
 
             def one(i, c):
@@ -376,7 +431,7 @@
     dtab[d] = dsend[d // per_w]
     prob_done = remote(dtab.at[pl.ds(0, n_bin - 1)], dtab.at[pl.ds(0, n_bin - 1)], d_ss, d_rs, sibling)
 
-    lax.fori_loop(2, nz + 1, step, 0)
+    lax.fori_loop(2, nz + HOLD, step, 0)
 
     prob_done.wait_recv()
     found = in_row(by_device(own_lanes(dtab[...]))[:, 0])
@@ -384,7 +439,7 @@
     found = (found[2:3] + found[1:2]) + found[0:1]
     prob_ref[...] = found[:, :part] + found[:, part:]
 
-    lax.fori_loop(nz + 1, nz + LAG, step, 0)
+    lax.fori_loop(nz + HOLD, nz + LAG, step, 0)
 
     def z_add(t, c):
         z_send(t).wait_recv()
@@ -397,8 +452,11 @@
     remote(all_stat, all_stat, s_ss, s_rs, sibling).wait_send()
     remote(all_sums, all_sums, b_ss, b_rs, sibling).wait_send()
     prob_done.wait_send()
+    for dx in steps_x:
+        head_all(dx).wait_send()
     for c, (m, n) in enumerate(chunks):
-        chunk_all(m, n, c).wait_send()
+        if c:
+            chunk_all(m, n, c).wait_send()
     for m in range(nd):
         for way in range(2):
             for h in range(2):
@@ -413,6 +471,11 @@
 
     lax.fori_loop(0, nz, v_done, 0)
     lax.fori_loop(0, nz - 1, lambda t, c: (z_send(t).wait_send(), c)[1], 0)
+
+
+def hand_on(a_ref, b_ref, c_ref, d_ref):
+    c_ref[...] = a_ref[...]
+    d_ref[...] = b_ref[...]
 
 
 def local(nz, images, bin_lists, precision, references, line_index, interp_blocks):
@@ -433,10 +496,12 @@
     prob, volume = pl.pallas_call(
         functools.partial(kernel, ny, nx, nz, nd, FAR),
         out_shape=(jax.ShapeDtypeStruct((1, part), F32), jax.ShapeDtypeStruct((LINE, LINE), F32)),
-        in_specs=[far, whole, whole, far, far, far],
+        in_specs=[far] * 6,
         out_specs=(whole, whole),
         scratch_shapes=[
             vmem((part, 2 * n_pair * CW), BF16),
+            vmem((2, part), I32),
+            vmem((1, part), BF16),
             vmem((rows, part), BF16),
             vmem((rows, 2 * part), BF16),
             vmem((n_ptcl, n_pair, 16, CW), BF16),
@@ -457,8 +522,9 @@
             vmem((nz, nx, LINE, LINE), F32),
             vmem((nz, nx - 1, LINE, LINE), BF16), vmem((nz, nx - 1, LINE, LINE), BF16),
             vmem((nz - 1, LINE, LINE), BF16), vmem((nz - 1, LINE, LINE), BF16),
-            dma((5,)),
+            dma((8,)),
             dma((n_pair,)), dma((n_pair,)), dma((n_pair,)),
+            dma((nx,)), dma((nx,)),
             dma(()), dma(()),
             dma((2, 2, nd)), dma((2, 2, nd)),
             dma((2, nd)), dma((2, nd)),
@@ -468,6 +534,12 @@
         compiler_params=pltpu.CompilerParams(collective_id=0, has_side_effects=True, vmem_limit_bytes=58 << 20),
         cost_estimate=pl.CostEstimate(flops=flops, bytes_accessed=n_ref * pixels * 2, transcendentals=0),
     )(images, bin_lists.T, precision.reshape(1, part), references[0], line_index[0].T, interp_blocks)
+    prob, volume = pl.pallas_call(
+        hand_on,
+        out_shape=(jax.ShapeDtypeStruct((1, part), F32), jax.ShapeDtypeStruct((LINE, LINE), F32)),
+        in_specs=[whole, whole],
+        out_specs=(whole, whole),
+    )(prob, volume)
     return prob.reshape(part, 1), volume[None]
 
 

time: 127 us -> 122 us (0.961); the launches traced: 124 us -> 121 us
  local copies, waits for them, and re-layouts: 2.59 us -> 0 us
    unnamed x2 -> x0, local copies, waits for them, and re-layouts: 2.59 us -> none
    pallas_call x1, Pallas kernels: 121 us -> 119 us  [local(): pl.pallas_call(functools.partial(kernel, ny, nx, nz, nd, FAR), out_shape=...]
    pallas_call x0 -> x1, Pallas kernels: none -> 1.48 us  [local(): pl.pallas_call(hand_on, out_shape=(jax.ShapeDtypeStruct((1, part), F32),...]
where the time goes in v4:
time: 122 us; the launch traced here: 121 us
  Pallas kernels  120 us (98%)
    pallas_call x1, Pallas kernels, local(): pl.pallas_call(functools.partial(kernel, ny, nx, nz, nd, FAR), out_shape=...  119 us

profile of v4, /device:TPU:8, one launch (start us, length us, event | category | flops | bytes accessed | tf_op | source)
XLA Modules:
  0.0 120.8 jit_solution(7319003551857546445)
XLA Ops:
  0.6 118.7 %shard_map.77 = (f32[1,128]{1,0:T(1,128)}, f32[128,128]{1,0:T(8,128)}) custom-call(bf16[128,8192]{1,0:T(8,128)(2,1)} %img_hbm.1, s32[2,128]{1,0:T(2,128)} %bitcast.11, bf16[1,128]{1,0:T(2,128)(2,1)} %bitcast.12, bf16[512,8192]{1,0:T(8,128)(2,1)} %bitcast.8, s32[64,512]{1,0:T(8,128)} %bitcast.9, bf16[64,128,128]{2,1,0:T(8,128)(2,1)} %interp_hbm.1), custom_call_target="tpu_custom_call" | custom-call | flops 8589934592 | bytes 8388608 | tf_op jit(solution)/shard_map/pallas_call | solution.py:496
  119.3 1.5 %shard_map.78 = (f32[1,128]{1,0:T(1,128)}, f32[128,128]{1,0:T(8,128)}) custom-call(f32[1,128]{1,0:T(1,128)} %get-tuple-element.6.a_ref, f32[128,128]{1,0:T(8,128)} %get-tuple-element.7.b_ref), custom_call_target="tpu_custom_call" | custom-call | tf_op jit(solution)/shard_map/pallas_call | solution.py:537

commit v5 on v4

--- a/solution.py
+++ b/solution.py
@@ -12,8 +12,8 @@
 NZ = 8
 CW = 128
 FAR = 4
-HOLD = 2
-LAG = 5
+HOLD = 1
+LAG = 4
 AHEAD = 5
 LINE = 128
 SLOTS = 8
@@ -37,10 +37,10 @@
 
 def kernel(ny, nx, nz, nd, far_n, img_hbm, bins_hbm, prec_hbm, refs_hbm, idx_hbm, interp_hbm, prob_ref, vol_ref,
            img, bins_ref, prec_ref, g, g2, sendbuf, recv, xs_all, refs, idx, onehot, interp, score, weight, hnorm,
-           psend, ptab, stat, lrow, ltab, dsend, dtab, vb, sib, xs, xr, zs, zr,
+           psend, ptab, stat, lrow, ltab, dsend, dtab, vb, sib, xs, xr, zs, zr, wr,
            load_sem, a_ss, a_rs, a_loc, h_ss, h_rs, p_ss, p_rs,
            y_ss, y_rs, f_ss, f_rs, s_ss, s_rs, b_ss, b_rs, d_ss, d_rs,
-           v_ss, v_rs, x_ss, x_rs, z_ss, z_rs):
+           v_ss, v_rs, x_ss, x_rs, z_ss, z_rs, w_ss, w_rs):
     nq = nx * nz
     y, d = lax.axis_index("cls"), lax.axis_index("ptcl")
     q, k = d // 2, d % 2
@@ -355,9 +355,25 @@
         x2 = (x + nx - 1 - i) % nx
         return remote(xs.at[t, i], xr.at[t, i], x_ss.at[t], x_rs.at[t], (y, (x2 * nz + z) * 2 + k))
 
-    def x_all(t):
-        ref = xr.at[t]
+    def x_all(t, n):
+        ref = xr.at[t, pl.ds(0, n)]
         return remote(ref, ref, x_ss.at[t], x_rs.at[t], sibling)
+
+    def is_near(t):
+        return (t < 2) | ((t >= nz - 3) & (t < nz - 1))
+
+    def w_send(t):
+        z2 = (z + nz - 1 - t) % nz
+        return remote(xs.at[t, 1], wr.at[t], w_ss.at[t], w_rs.at[t], (y, (x * nz + z2) * 2 + k))
+
+    def x_wait(t, kind):
+        @pl.when(is_near(t))
+        def _():
+            getattr(x_all(t, nx - 2), kind)()
+
+        @pl.when(jnp.logical_not(is_near(t)))
+        def _():
+            getattr(x_all(t, nx - 1), kind)()
 
     def z_send(t):
         z2 = (z + nz - 1 - t) % nz
@@ -392,18 +408,36 @@
 
             def one(i, c):
                 xs[u, i] = (vb[u, i, k] + sib[u, i]).astype(BF16)
-                x_send(u, i).start()
+
+                @pl.when((i != 1) | jnp.logical_not(is_near(u) | (u == nz - 1)))
+                def _():
+                    x_send(u, i).start()
+
+                @pl.when((i == 1) & is_near(u))
+                def _():
+                    w_send(u).start()
+
                 return c
 
             lax.fori_loop(0, nx - 1, one, 0)
+
+        @pl.when(t == nz + HOLD)
+        def _():
+            total = vb[nz - 1, 1, k] + sib[nz - 1, 1]
+            for u in (0, 1, nz - 3, nz - 2):
+                w_send(u).wait_recv()
+                total += wr[u].astype(F32)
+            xs[nz - 1, 1] = total.astype(BF16)
+            x_send(nz - 1, 1).start()
 
         @pl.when(t >= LAG)
         def _():
             u = t - LAG
-            x_all(u).wait_recv()
+            x_wait(u, "wait_recv")
             total = vb[u, nx - 1, k] + sib[u, nx - 1]
-            for i in range(nx - 1):
+            for i in (0, 2):
                 total += xr[u, i].astype(F32)
+            total += jnp.where(is_near(u), 0.0, xr[u, 1].astype(F32))
 
             @pl.when(u < nz - 1)
             def _():
@@ -466,10 +500,12 @@
 
     def v_done(t, c):
         sib_send(t).wait_send()
-        x_all(t).wait_send()
+        x_wait(t, "wait_send")
         return c
 
     lax.fori_loop(0, nz, v_done, 0)
+    for u in (0, 1, nz - 3, nz - 2):
+        w_send(u).wait_send()
     lax.fori_loop(0, nz - 1, lambda t, c: (z_send(t).wait_send(), c)[1], 0)
 
 
@@ -522,6 +558,7 @@
             vmem((nz, nx, LINE, LINE), F32),
             vmem((nz, nx - 1, LINE, LINE), BF16), vmem((nz, nx - 1, LINE, LINE), BF16),
             vmem((nz - 1, LINE, LINE), BF16), vmem((nz - 1, LINE, LINE), BF16),
+            vmem((nz, LINE, LINE), BF16),
             dma((8,)),
             dma((n_pair,)), dma((n_pair,)), dma((n_pair,)),
             dma((nx,)), dma((nx,)),
@@ -529,7 +566,7 @@
             dma((2, 2, nd)), dma((2, 2, nd)),
             dma((2, nd)), dma((2, nd)),
             dma(()), dma(()), dma(()), dma(()), dma(()), dma(()),
-            dma((nz,)), dma((nz,)), dma((nz,)), dma((nz,)), dma((nz - 1,)), dma((nz - 1,)),
+            dma((nz,)), dma((nz,)), dma((nz,)), dma((nz,)), dma((nz - 1,)), dma((nz - 1,)), dma((nz,)), dma((nz,)),
         ],
         compiler_params=pltpu.CompilerParams(collective_id=0, has_side_effects=True, vmem_limit_bytes=58 << 20),
         cost_estimate=pl.CostEstimate(flops=flops, bytes_accessed=n_ref * pixels * 2, transcendentals=0),

time: 122 us -> 121 us (level)
  no operation moved by 1% of the time
where the time goes in v5:
time: 121 us; the launch traced here: 120 us
  Pallas kernels  119 us (98%)
    pallas_call x1, Pallas kernels, local(): pl.pallas_call(functools.partial(kernel, ny, nx, nz, nd, FAR), out_shape=...  118 us

profile of v5, /device:TPU:8, one launch (start us, length us, event | category | flops | bytes accessed | tf_op | source)
XLA Modules:
  0.0 120.0 jit_solution(13912139446374490997)
XLA Ops:
  0.6 117.9 %shard_map.77 = (f32[1,128]{1,0:T(1,128)}, f32[128,128]{1,0:T(8,128)}) custom-call(bf16[128,8192]{1,0:T(8,128)(2,1)} %img_hbm.1, s32[2,128]{1,0:T(2,128)} %bitcast.11, bf16[1,128]{1,0:T(2,128)(2,1)} %bitcast.12, bf16[512,8192]{1,0:T(8,128)(2,1)} %bitcast.8, s32[64,512]{1,0:T(8,128)} %bitcast.9, bf16[64,128,128]{2,1,0:T(8,128)(2,1)} %interp_hbm.1), custom_call_target="tpu_custom_call" | custom-call | flops 8589934592 | bytes 8388608 | tf_op jit(solution)/shard_map/pallas_call | solution.py:532
  118.5 1.5 %shard_map.78 = (f32[1,128]{1,0:T(1,128)}, f32[128,128]{1,0:T(8,128)}) custom-call(f32[1,128]{1,0:T(1,128)} %get-tuple-element.6.a_ref, f32[128,128]{1,0:T(8,128)} %get-tuple-element.7.b_ref), custom_call_target="tpu_custom_call" | custom-call | tf_op jit(solution)/shard_map/pallas_call | solution.py:574
